TPU v7x, 512 devices: a whole 4x8x8 slice. The times are simulated.
512 devices in a mesh: seq: 32 (over z, x), head: 16 (over y, core).
Axes of the slice: x: 4, y: 8, z: 8, core: 2. Of those that a mesh axis runs over, the one named last changes fastest.
Arguments:
- projected: bfloat16 [65536, 3072], P(('seq', 'head')), may hold values from -28 to 28, as said below
- upstream: bfloat16 [65536, 768], P(('seq', 'head')), may hold values from -6 to 6
- out_weight: bfloat16 [768, 768], replicated, may hold values from -0.21875 to 0.21875
- tile_weights: bfloat16 [1536, 128, 128], P('seq'), may hold values from -0.5 to 0.5
- tile_owner: int32 [1536, 1], replicated, may hold values from 0 to 31; in each aligned block of 48 rows (0 to 47, 48 to 95, ...) at most 3 rows name the same one
- source_block: int32 [1536], replicated, may hold values from 0 to 15
- target_block: int32 [1536], replicated, may hold values from 0 to 15
- key_blocks: int32 [512, 4], P('seq'), may hold values from 0 to 15, as said below
- key_count: int32 [512], P('seq'), may hold values from 1 to 4, as said below
Outputs:
- layer_out: bfloat16 [65536, 768], P(('seq', 'head'))
- grad_projected: bfloat16 [65536, 3072], P(('seq', 'head'))
- weight_grad: float32 [768, 768], P('head', 'seq')
Inputs may be any that keep to these rules, and one draw needn't show every extreme that they name: `projected`: queries and keys carry the scale of the score. `key_blocks`: row r lists distinct blocks, its own block r % 16 first. `key_count`: every shard has a query block that attends 4 key blocks. `tile_owner`: among the 48 tiles of one shard no owner is named more than 3 times, a bound that some block reaches.
All inputs are finite; a program needn't handle non-finite values.
Results may differ from a plain program's by a relative error of at most 0.0057.
Values may be sent and summed in bfloat16 or wider, within the bound.
A program may use at most 64 MiB of HBM per device.

v0:
```python
import math

import jax
import jax.numpy as jnp
from jax import lax
from jax.sharding import PartitionSpec as P

HEADS = 16
BLOCK = 128
CAP = 3


finest = lax.Precision.HIGHEST


def attend(query_rows, key_rows, value_rows, grad_rows, block_lists, block_counts):
    block_total, block_size, head_count, head_size = query_rows.shape
    slot_total = block_lists.shape[1]
    score_scale = head_size ** (-0.5)
    group_size = math.gcd(block_total, max(1, 512 // block_size))
    slot_ids = jnp.arange(slot_total, dtype=jnp.int32)
    usable_all = slot_ids[None, :] < block_counts[:, None]
    onehot_all = (
        (block_lists[:, :, None] == jnp.arange(block_total, dtype=jnp.int32)[None, None, :])
        & usable_all[:, :, None]
    ).astype(jnp.float32)

    def advance(running, step_index):
        acc_keys, acc_values = running
        first_block = step_index * group_size
        query_part = lax.dynamic_slice_in_dim(query_rows, first_block, group_size, 0)
        grad_part = lax.dynamic_slice_in_dim(grad_rows, first_block, group_size, 0)
        chosen = lax.dynamic_slice_in_dim(block_lists, first_block, group_size, 0)
        usable = lax.dynamic_slice_in_dim(usable_all, first_block, group_size, 0)
        onehot_part = lax.dynamic_slice_in_dim(onehot_all, first_block, group_size, 0)
        near_keys = key_rows[chosen]
        near_values = value_rows[chosen]
        scores = (
            jnp.einsum(
                "gihd,gjkhd->ghijk", query_part, near_keys, preferred_element_type=jnp.float32
            )
            * score_scale
        )
        scores = jnp.where(usable[:, None, None, :, None], scores, -jnp.inf)
        maximum = jnp.max(scores, axis=(3, 4), keepdims=True)
        exponent = jnp.exp(scores - maximum)
        probability = exponent / jnp.sum(exponent, axis=(3, 4), keepdims=True)
        probability_b = probability.astype(jnp.bfloat16)
        output = jnp.einsum(
            "ghijk,gjkhd->gihd", probability_b, near_values, preferred_element_type=jnp.float32
        ).astype(jnp.bfloat16)
        grad_prob = jnp.einsum(
            "gihd,gjkhd->ghijk", grad_part, near_values, preferred_element_type=jnp.float32
        )
        row_delta = jnp.sum(probability * grad_prob, axis=(3, 4), keepdims=True)
        dscore = (probability * (grad_prob - row_delta) * score_scale).astype(jnp.bfloat16)
        grad_query = jnp.einsum(
            "ghijk,gjkhd->gihd", dscore, near_keys, preferred_element_type=jnp.float32
        ).astype(jnp.bfloat16)
        key_terms = jnp.einsum(
            "ghijk,gihd->gjkhd", dscore, query_part, preferred_element_type=jnp.float32
        )
        value_terms = jnp.einsum(
            "ghijk,gihd->gjkhd", probability_b, grad_part, preferred_element_type=jnp.float32
        )
        acc_keys = acc_keys + jnp.einsum(
            "gjb,gjkhd->bkhd", onehot_part, key_terms, precision=finest
        )
        acc_values = acc_values + jnp.einsum(
            "gjb,gjkhd->bkhd", onehot_part, value_terms, precision=finest
        )
        return ((acc_keys, acc_values), (output, grad_query))

    zero_grad = jnp.zeros(query_rows.shape, jnp.float32)
    (acc_keys, acc_values), (outputs, grad_queries) = lax.scan(
        advance, (zero_grad, zero_grad), jnp.arange(block_total // group_size, dtype=jnp.int32)
    )
    return (
        outputs.reshape(query_rows.shape),
        grad_queries.reshape(query_rows.shape),
        acc_keys.astype(jnp.bfloat16),
        acc_values.astype(jnp.bfloat16),
    )


def body(
    projected,
    upstream,
    out_weight,
    tile_weights,
    tile_owner,
    source_block,
    target_block,
    key_blocks,
    key_count,
):
    node_rows, width = upstream.shape
    head_groups = lax.axis_size("head")
    shards = lax.axis_size("seq")
    local_heads = HEADS // head_groups
    head_size = width // HEADS
    shard_rows = node_rows * head_groups
    blocks = shard_rows // BLOCK
    lane_width = local_heads * head_size
    seq_index = lax.axis_index("seq")
    grad_attention = jnp.einsum(
        "nd,ed->ne", upstream, out_weight, preferred_element_type=jnp.float32
    ).astype(jnp.bfloat16)
    extra_columns = jnp.stack(
        [
            grad_attention.reshape(node_rows, HEADS, head_size),
            upstream.reshape(node_rows, HEADS, head_size),
        ],
        axis=2,
    ).reshape(node_rows, HEADS * 2 * head_size)
    arrived_heads, arrived_extra = (
        lax.all_to_all(projected, "head", split_axis=1, concat_axis=0, tiled=True),
        lax.all_to_all(extra_columns, "head", split_axis=1, concat_axis=0, tiled=True),
    )
    arrived_extra = arrived_extra.reshape(shard_rows, local_heads, 2, head_size)
    grad_heads = arrived_extra[:, :, 0, :]
    grad_mixed = arrived_extra[:, :, 1, :].reshape(shard_rows, lane_width)
    arrived_heads = arrived_heads.reshape(shard_rows, local_heads, 4, head_size)

    def blocked(array):
        return array.reshape(blocks, BLOCK, local_heads, head_size)

    attended, grad_query, grad_key, grad_value = attend(
        blocked(arrived_heads[:, :, 0, :]),
        blocked(arrived_heads[:, :, 1, :]),
        blocked(arrived_heads[:, :, 2, :]),
        blocked(grad_heads),
        key_blocks,
        key_count,
    )
    per_shard = tile_weights.shape[0]
    block_span = BLOCK * lane_width
    slot_total = shards * CAP
    slot_range = jnp.arange(slot_total, dtype=jnp.int32)
    block_range = jnp.arange(blocks, dtype=jnp.int32)
    owners = tile_owner[:, 0].reshape(shards, per_shard)
    owner_seen = (owners[:, :, None] == jnp.arange(shards, dtype=jnp.int32)[None, None, :]).astype(
        jnp.int32
    )
    tile_ranks = jnp.sum((jnp.cumsum(owner_seen, axis=1) - 1) * owner_seen, axis=2)
    my_owners = lax.dynamic_index_in_dim(owners, seq_index, 0, keepdims=False)
    my_ranks = lax.dynamic_index_in_dim(tile_ranks, seq_index, 0, keepdims=False)
    placement = ((my_owners * CAP + my_ranks)[:, None] == slot_range[None, :]).astype(jnp.bfloat16)
    my_sources = lax.dynamic_slice_in_dim(source_block, seq_index * per_shard, per_shard, 0)
    source_onehot = (my_sources[:, None] == block_range[None, :]).astype(jnp.bfloat16)
    feature_blocks = arrived_heads[:, :, 3, :].reshape(blocks, block_span)
    picked = (
        jnp.dot(source_onehot, feature_blocks, preferred_element_type=jnp.float32)
        .astype(jnp.bfloat16)
        .reshape(per_shard, BLOCK, lane_width)
    )
    partials = jnp.einsum(
        "tij,tjw->tiw", tile_weights, picked, preferred_element_type=jnp.float32
    ).astype(jnp.bfloat16)
    outgoing = (
        jnp.einsum(
            "tp,tx->px",
            placement,
            partials.reshape(per_shard, block_span),
            preferred_element_type=jnp.float32,
        )
        .astype(jnp.bfloat16)
        .reshape(shards, CAP, block_span)
    )
    incoming_slot = jnp.arange(shards, dtype=jnp.int32)[:, None] * CAP + tile_ranks
    incoming_onehot = (
        (incoming_slot[:, :, None] == slot_range[None, None, :]) & (owners == seq_index)[:, :, None]
    ).astype(jnp.float32)
    target_onehot = (
        target_block.reshape(shards, per_shard)[:, :, None] == block_range[None, None, :]
    ).astype(jnp.float32)
    receive_map = jnp.einsum(
        "stp,stb->pb", incoming_onehot, target_onehot, precision=finest
    ).astype(jnp.bfloat16)
    replies = (
        jnp.dot(
            receive_map, grad_mixed.reshape(blocks, block_span), preferred_element_type=jnp.float32
        )
        .astype(jnp.bfloat16)
        .reshape(shards, CAP, block_span)
    )
    arrived, returned = (
        lax.all_to_all(outgoing, "seq", split_axis=0, concat_axis=0, tiled=True),
        lax.all_to_all(replies, "seq", split_axis=0, concat_axis=0, tiled=True),
    )
    mixed_blocks = jnp.einsum(
        "pb,px->bx",
        receive_map,
        arrived.reshape(slot_total, block_span),
        preferred_element_type=jnp.float32,
    ).astype(jnp.bfloat16)
    returned_blocks = (
        jnp.dot(
            placement, returned.reshape(slot_total, block_span), preferred_element_type=jnp.float32
        )
        .astype(jnp.bfloat16)
        .reshape(per_shard, BLOCK, lane_width)
    )
    back_terms = jnp.einsum(
        "tij,tiw->tjw", tile_weights, returned_blocks, preferred_element_type=jnp.float32
    )
    grad_features = jnp.einsum(
        "tb,tx->bx",
        source_onehot.astype(jnp.float32),
        back_terms.reshape(per_shard, block_span),
        precision=finest,
    ).astype(jnp.bfloat16)
    heads_shape = (shard_rows, local_heads, head_size)
    combined = jnp.stack(
        [attended.reshape(heads_shape), mixed_blocks.reshape(heads_shape)], axis=2
    ).reshape(shard_rows, 2 * lane_width)
    grads_heads = jnp.stack(
        [
            grad_query.reshape(heads_shape),
            grad_key.reshape(heads_shape),
            grad_value.reshape(heads_shape),
            grad_features.reshape(heads_shape),
        ],
        axis=2,
    ).reshape(shard_rows, 4 * lane_width)
    node_combined, grad_projected = (
        lax.all_to_all(combined, "head", split_axis=0, concat_axis=1, tiled=True),
        lax.all_to_all(grads_heads, "head", split_axis=0, concat_axis=1, tiled=True),
    )
    node_combined = node_combined.reshape(node_rows, HEADS, 2, head_size)
    attention_nodes = node_combined[:, :, 0, :].reshape(node_rows, width)
    mixed_nodes = node_combined[:, :, 1, :].reshape(node_rows, width)
    layer_out = (
        jnp.dot(attention_nodes, out_weight, preferred_element_type=jnp.float32)
        + mixed_nodes.astype(jnp.float32)
    ).astype(jnp.bfloat16)
    total_nodes = shard_rows * shards
    partial_grad = jnp.einsum(
        "nd,ne->de", attention_nodes, upstream, preferred_element_type=jnp.float32
    )
    row_part = width // head_groups
    column_part = width // shards
    arranged = (
        partial_grad.reshape(head_groups, row_part, shards, column_part)
        .transpose(2, 0, 1, 3)
        .reshape(shards * head_groups, row_part, column_part)
    )
    summed = lax.psum_scatter(arranged, ("seq", "head"), scatter_dimension=0, tiled=True).reshape(
        row_part, column_part
    )
    weight_grad = summed * (1.0 / math.sqrt(total_nodes))
    return (layer_out, grad_projected, weight_grad)


def solution(mesh):
    in_specs = (
        P(("seq", "head"), None),
        P(("seq", "head"), None),
        P(),
        P("seq", None, None),
        P(),
        P(),
        P(),
        P("seq", None),
        P("seq"),
    )
    out_specs = (P(("seq", "head"), None), P(("seq", "head"), None), P("head", "seq"))
    return jax.shard_map(body, mesh=mesh, in_specs=in_specs, out_specs=out_specs, check_vma=False)
```

profile of v0, /device:TPU:1, one launch (start us, length us, event | category | flops | bytes accessed | tf_op | source)
XLA Modules:
  0.0 527.5 jit_solution(1287698378287156206)
XLA Ops:
  8.4 2.0 convolution_convert_fusion.7
  11.4 10.2 %all-to-all-start.1 = ((bf16[128,16,96]{0,2,1:T(8,128)(2,1)}), bf16[128,16,96]{0,2,1:T(8,128)(2,1)S(1)}, u32[]{:S(2)}, u32[]{:S(2)}) async-start(bf16[128,16,96]{0,2,1:T(8,128)(2,1)} %bitcast.4), calls=%async_computation.1 | async-start | bytes 786432 | tf_op jit(solution)/shard_map/all_to_all | solution.py:118
  23.0 1.3 select_reduce_fusion
  24.4 11.7 %all-to-all-done.1 = bf16[128,16,96]{0,2,1:T(8,128)(2,1)S(1)} async-done(((bf16[128,16,96]{0,2,1:T(8,128)(2,1)}), bf16[128,16,96]{0,2,1:T(8,128)(2,1)S(1)}, u32[]{:S(2)}, u32[]{:S(2)}) %all-to-all-start.1) | async-done | bytes 393248 | tf_op jit(solution)/shard_map/all_to_all | solution.py:118
  36.2 3.5 all-to-all-start
  41.8 1.5 reshape_reshape_squeeze.3
  43.3 1.4 convolution_convert_fusion
  44.7 2.1 reshape.213
  46.8 15.0 %all-to-all-done = bf16[128,16,192]{0,2,1:T(8,128)(2,1)S(1)} async-done(((bf16[128,16,192]{0,2,1:T(8,128)(2,1)}), bf16[128,16,192]{0,2,1:T(8,128)(2,1)S(1)}, u32[]{:S(2)}, u32[]{:S(2)}) %all-to-all-start) | async-done | bytes 786464 | tf_op jit(solution)/shard_map/all_to_all | solution.py:117
  61.7 11.5 %all-to-all-start.4 = ((bf16[32,3,6144]{2,1,0:T(4,128)(2,1)}), bf16[32,3,6144]{2,1,0:T(4,128)(2,1)}, u32[]{:S(2)}, u32[]{:S(2)}) async-start(bf16[32,3,6144]{2,1,0:T(4,128)(2,1)} %reshape.213), calls=%async_computation.4 | async-start | bytes 3145728 | tf_op jit(solution)/shard_map/all_to_all | solution.py:189
  75.9 1.4 copy.150
  77.3 1.4 reshape.206
  81.7 2.5 reshape.208
  84.3 1.8 fusion.22
  86.1 1.7 copy.166
  87.8 3.6 reshape.209
  91.4 1.6 convolution_convert_fusion.1
  93.0 2.1 reshape.210
  96.6 14.7 %all-to-all-done.4 = bf16[32,3,6144]{2,1,0:T(4,128)(2,1)} async-done(((bf16[32,3,6144]{2,1,0:T(4,128)(2,1)}), bf16[32,3,6144]{2,1,0:T(4,128)(2,1)}, u32[]{:S(2)}, u32[]{:S(2)}) %all-to-all-start.4) | async-done | bytes 1179680 | tf_op jit(solution)/shard_map/all_to_all | solution.py:189
  111.4 6.0 %all-to-all-start.2 = ((bf16[32,3,6144]{2,1,0:T(4,128)(2,1)}), bf16[32,3,6144]{2,1,0:T(4,128)(2,1)}, u32[]{:S(2)}, u32[]{:S(2)}) async-start(bf16[32,3,6144]{2,1,0:T(4,128)(2,1)} %reshape.210), calls=%async_computation.2 | async-start | bytes 3145728 | tf_op jit(solution)/shard_map/all_to_all | solution.py:188
  117.4 55.9 %while.17 = (s32[]{:T(128)}, f32[16,128,1,48]{1,0,3,2:T(8,128)}, f32[16,128,1,48]{1,0,3,2:T(8,128)}, bf16[4,4,128,1,48]{2,1,0,4,3:T(4,128)(2,1)}, bf16[4,4,128,1...) while((s32[]{:T(128)}, f32[16,128,1,48]{1,0,3,2:T(8,128)}, ...), condition=%wide.region_4.5_spmd.clone, body=%wide.region_0.4_spmd.clone.sunk | while | flops 194690608 | bytes 18972772 | solution.py:75
  121.5 1.5 gather_fusion.1
  126.9 2.5 fusion.102
  135.3 1.5 gather_fusion.1
  140.8 2.6 fusion.102
  149.3 1.5 gather_fusion.1
  154.8 2.6 fusion.102
  163.3 1.5 gather_fusion.1
  168.8 2.6 fusion.102
  177.8 2.8 reshape.214
  181.8 2.5 reshape.215
  184.3 3.9 reshape.211
  188.3 1.5 convolution_convert_fusion.5
  189.8 1.4 stack_reshape.20
  193.4 4.7 all-to-all-start.3
  198.1 1.6 convolution_bitcast_fusion.7
  199.7 3.2 copy.173
  202.9 3.7 reshape.216
  207.8 1.5 stack_reshape.23
  210.9 1.7 all-to-all-done.3
  213.4 5.5 %all-to-all-start.5 = ((bf16[16,128,192]{1,2,0:T(8,128)(2,1)}), bf16[16,128,192]{1,2,0:T(8,128)(2,1)S(1)}, u32[]{:S(2)}, u32[]{:S(2)}) async-start(bf16[16,128,192]{1,2,0:T(8,128)(2,1)} %copy.175), calls=%async_computation.5 | async-start | bytes 1572864 | tf_op jit(solution)/shard_map/all_to_all | solution.py:228
  219.2 1.9 convolution_bitcast_fusion.6
  221.2 6.3 %copy.178 = f32[32,16,48,24]{2,3,1,0:T(8,128)} copy(f32[32,16,48,24]{2,0,3,1:T(8,128)S(1)} %convolution_bitcast_fusion.6) | data formatting | bytes 4718592 | tf_op jit(solution)/shard_map/transpose | solution.py:245
  229.9 1.9 copy.169
  231.9 9.7 %all-to-all-done.5 = bf16[16,128,192]{1,2,0:T(8,128)(2,1)S(1)} async-done(((bf16[16,128,192]{1,2,0:T(8,128)(2,1)}), bf16[16,128,192]{1,2,0:T(8,128)(2,1)S(1)}, u32[]{:S(2)}, u32[]{:S(2)}) %all-to-all-start.5) | async-done | bytes 786464 | tf_op jit(solution)/shard_map/all_to_all | solution.py:228
  242.7 2.1 fusion.23
  244.9 274.4 %all-reduce.3.cloned.1.call-done = f32[512,48,24]{1,2,0:T(8,128)} async-done(((f32[512,48,24]{1,2,0:T(8,128)}), f32[512,48,24]{1,2,0:T(8,128)}) %all-reduce.3.cloned.1.call-update) | async-done | bytes 2359312
  519.3 1.3 fusion.38
  (260 shorter events, 64.5 us)
Async XLA Ops:
  7.2 77.1 %copy-start = (bf16[48,128,128]{2,1,0:T(8,128)(2,1)S(1)}, bf16[48,128,128]{2,1,0:T(8,128)(2,1)}, u32[]{:S(2)}) copy-start(bf16[48,128,128]{2,1,0:T(8,128)(2,1)} %param.14) | copy-start | bytes 4718596
  8.4 3.0 copy-start.9
  10.4 11.2 %copy-start.15 = (bf16[128,3072]{1,0:T(8,128)(2,1)S(1)}, bf16[128,3072]{1,0:T(8,128)(2,1)}, u32[]{:S(2)}) copy-start(bf16[128,3072]{1,0:T(8,128)(2,1)} %param.11) | copy-start | bytes 2359300
  10.6 12.2 %copy-start.28 = (s32[1536,1]{0,1:T(1,128)S(1)}, s32[1536,1]{0,1:T(1,128)}, u32[]{:S(2)}) copy-start(s32[1536,1]{0,1:T(1,128)} %param.15) | copy-start | bytes 18436
  10.6 13.8 %copy-start.25 = (s32[1536]{0:T(1024)S(1)}, s32[1536]{0:T(1024)}, u32[]{:S(2)}) copy-start(s32[1536]{0:T(1024)} %param.17) | copy-start | bytes 18436
  11.4 24.8 %all-to-all-start.1 = ((bf16[128,16,96]{0,2,1:T(8,128)(2,1)}), bf16[128,16,96]{0,2,1:T(8,128)(2,1)S(1)}, u32[]{:S(2)}, u32[]{:S(2)}) async-start(bf16[128,16,96]{0,2,1:T(8,128)(2,1)} %bitcast.4), calls=%async_computation.1 | async-start | bytes 786432 | tf_op jit(solution)/shard_map/all_to_all | solution.py:118
  23.0 17.5 %copy-start.18 = (s32[32,48]{0,1:T(8,128)}, s32[32,48]{0,1:T(8,128)S(1)}, u32[]{:S(2)}) copy-start(s32[32,48]{0,1:T(8,128)S(1)} %copy.161) | copy-start | bytes 18436
  24.3 16.2 %copy-start.20 = (s32[32,48]{0,1:T(8,128)}, s32[32,48]{0,1:T(8,128)S(1)}, u32[]{:S(2)}) copy-start(s32[32,48]{0,1:T(8,128)S(1)} %select_reduce_fusion) | copy-start | bytes 18436
  36.2 25.6 %all-to-all-start = ((bf16[128,16,192]{0,2,1:T(8,128)(2,1)}), bf16[128,16,192]{0,2,1:T(8,128)(2,1)S(1)}, u32[]{:S(2)}, u32[]{:S(2)}) async-start(bf16[128,16,192]{0,2,1:T(8,128)(2,1)} %bitcast), calls=%async_computation | async-start | bytes 1572864 | tf_op jit(solution)/shard_map/all_to_all | solution.py:117
  46.8 26.6 %copy-start.33 = (s32[16,4]{0,1:T(4,128)S(1)}, s32[16,4]{0,1:T(4,128)}, u32[]{:S(2)}) copy-start(s32[16,4]{0,1:T(4,128)} %param.18) | copy-start | bytes 772
  46.8 27.4 %copy-start.19 = (s32[32,48]{0,1:T(8,128)S(1)}, s32[32,48]{0,1:T(8,128)}, u32[]{:S(2)}) copy-start(s32[32,48]{0,1:T(8,128)} %copy-done.18) | copy-start | bytes 18436
  46.8 27.4 %copy-start.21 = (s32[32,48]{0,1:T(8,128)S(1)}, s32[32,48]{0,1:T(8,128)}, u32[]{:S(2)}) copy-start(s32[32,48]{0,1:T(8,128)} %copy-done.20) | copy-start | bytes 18436
  46.8 27.6 %copy-start.34 = (s32[16]{0:T(128)S(1)}, s32[16]{0:T(128)}, u32[]{:S(2)}) copy-start(s32[16]{0:T(128)} %param.19) | copy-start | bytes 196
  46.8 28.4 %copy-start.16 = (bf16[6,8,16,128]{3,1,2,0:T(8,128)(2,1)S(1)}, bf16[6,8,16,128]{3,1,2,0:T(8,128)(2,1)}, u32[]{:S(2)}) copy-start(bf16[6,8,16,128]{3,1,2,0:T(8,128)(2,1)} %get-tuple-element.233) | copy-start | bytes 589828
  61.7 49.6 %all-to-all-start.4 = ((bf16[32,3,6144]{2,1,0:T(4,128)(2,1)}), bf16[32,3,6144]{2,1,0:T(4,128)(2,1)}, u32[]{:S(2)}, u32[]{:S(2)}) async-start(bf16[32,3,6144]{2,1,0:T(4,128)(2,1)} %reshape.213), calls=%async_computation.4 | async-start | bytes 3145728 | tf_op jit(solution)/shard_map/all_to_all | solution.py:189
  74.2 6.4 %copy-start.31 = (s32[48]{0:T(128)}, s32[48]{0:T(128)S(1)}, u32[]{:S(2)}) copy-start(s32[48]{0:T(128)S(1)} %dynamic_slice.31) | copy-start | bytes 580
  74.4 17.0 %copy-start.29 = (s32[48]{0:T(128)}, s32[48]{0:T(128)S(1)}, u32[]{:S(2)}) copy-start(s32[48]{0:T(128)S(1)} %add_reduce_fusion) | copy-start | bytes 580
  111.4 73.0 %all-to-all-start.2 = ((bf16[32,3,6144]{2,1,0:T(4,128)(2,1)}), bf16[32,3,6144]{2,1,0:T(4,128)(2,1)}, u32[]{:S(2)}, u32[]{:S(2)}) async-start(bf16[32,3,6144]{2,1,0:T(4,128)(2,1)} %reshape.210), calls=%async_computation.2 | async-start | bytes 3145728 | tf_op jit(solution)/shard_map/all_to_all | solution.py:188
  117.4 2.9 copy-start.26
  125.9 3.6 copy-start.5
  126.9 4.4 copy-start.27
  126.9 4.4 copy-start.36
  131.3 2.9 copy-start.26
  139.7 3.7 copy-start.5
  140.8 2.9 copy-start.1
  140.8 4.5 copy-start.27
  140.8 4.5 copy-start.36
  145.3 2.9 copy-start.26
  153.7 3.7 copy-start.5
  154.8 2.9 copy-start.1
  154.8 4.5 copy-start.27
  154.8 4.5 copy-start.36
  167.7 3.7 copy-start.5
  168.8 2.9 copy-start.1
  168.8 4.5 copy-start.27
  168.8 4.5 copy-start.36
  173.2 2.9 copy-start.3
  173.2 3.7 copy-start.22
  177.0 3.6 copy-start.30
  184.3 4.0 copy-start.24
  193.4 19.2 %all-to-all-start.3 = ((bf16[16,128,96]{1,2,0:T(8,128)(2,1)}), bf16[16,128,96]{1,2,0:T(8,128)(2,1)S(1)}, u32[]{:S(2)}, u32[]{:S(2)}) async-start(bf16[16,128,96]{1,2,0:T(8,128)(2,1)} %copy.168), calls=%async_computation.3 | async-start | bytes 786432 | tf_op jit(solution)/shard_map/all_to_all | solution.py:227
  202.9 3.7 copy-start.32
  206.6 3.0 copy-start.11
  206.6 3.0 copy-start.12
  209.8 9.4 %copy-start.10 = (bf16[128,768]{0,1:T(8,128)(2,1)S(1)}, bf16[128,768]{0,1:T(8,128)(2,1)}, u32[]{:S(2)}) copy-start(bf16[128,768]{0,1:T(8,128)(2,1)} %copy-done.9) | copy-start | bytes 589828
  213.4 28.2 %all-to-all-start.5 = ((bf16[16,128,192]{1,2,0:T(8,128)(2,1)}), bf16[16,128,192]{1,2,0:T(8,128)(2,1)S(1)}, u32[]{:S(2)}, u32[]{:S(2)}) async-start(bf16[16,128,192]{1,2,0:T(8,128)(2,1)} %copy.175), calls=%async_computation.5 | async-start | bytes 1572864 | tf_op jit(solution)/shard_map/all_to_all | solution.py:228
  218.9 300.4 %all-reduce.3.cloned.1.call-start = ((), (), s32[]{:S(2)}) async-start(), calls=%async_computation.6 | async-start | bytes 12582912
  229.1 13.6 %copy-start.6 = (bf16[768,768]{1,0:T(8,128)(2,1)S(1)}, bf16[768,768]{1,0:T(8,128)(2,1)}, u32[]{:S(2)}) copy-start(bf16[768,768]{1,0:T(8,128)(2,1)} %param.13) | copy-start | bytes 3538948
  (23 other events, 35.3 us)
Sparse Core Ops, SparseCore 0:
  227.6 291.6 all-reduce.2
where the time goes:
time: 530 us; the launch traced here: 527 us
  waiting for transfers between devices  327 us (62%)
  local copies, waits for them, and re-layouts  90.7 us (17%)
  matrix products  42.4 us (8%)
  starting transfers between devices  41.8 us (8%)
  between operations  14.6 us (3%)
  other arithmetic  7.61 us (1%)
    unnamed x2, waiting for transfers between devices  274 us
    all_to_all x1, waiting for transfers between devices, body(): lax.all_to_all(projected, 'head', split_axis=1, concat_axis=0, tiled=True)  15 us
    all_to_all x1, waiting for transfers between devices, body(): lax.all_to_all(replies, 'seq', split_axis=0, concat_axis=0, tiled=True)  14.7 us
    all_to_all x1, waiting for transfers between devices, body(): lax.all_to_all(extra_columns, 'head', split_axis=1, concat_axis=0, tiled=...  11.7 us
    all_to_all x1, starting transfers between devices, body(): lax.all_to_all(replies, 'seq', split_axis=0, concat_axis=0, tiled=True)  11.5 us
  transfers between devices with their start and end apart: 7, of which 6 were waited for; matrix products, arithmetic and copies ran while one was open for 23% of the time, Pallas kernels for 0%

commit v1 on v0

v1 whole, which is shorter than its diff:
```python
import functools
import math

import jax
import jax.numpy as jnp
from jax import lax
from jax.experimental import pallas as pl
from jax.experimental.pallas import tpu as pltpu
from jax.sharding import PartitionSpec as P

MESH = pl.DeviceIdType.MESH
HEADS = 16
BLOCK = 128
CAP = 3
HS = 48
D = 768
QB = 16
KMAX = 4
TILES = 48
SHARDS = 32
SLOTS = SHARDS * CAP
NX = 4
NZ = 8
F32 = jnp.float32
BF16 = jnp.bfloat16

T_TILE_OF = 0
T_SRC = T_TILE_OF + SLOTS
T_SLOT_OF = T_SRC + TILES
T_PREV_SRC = T_SLOT_OF + TILES
T_LAST_SRC = T_PREV_SRC + TILES
T_REPLY = T_LAST_SRC + QB
T_PREV_TGT = T_REPLY + SLOTS
T_LAST_TGT = T_PREV_TGT + SLOTS
T_KEY = T_LAST_TGT + QB
T_COUNT = T_KEY + QB * KMAX
T_PREV_KEY = T_COUNT + QB
T_LAST_KEY = T_PREV_KEY + QB * KMAX
T_ALL = T_LAST_KEY + QB


def nn(a, b):
    return lax.dot_general(a, b, (((1,), (0,)), ((), ())), preferred_element_type=F32)


def nt(a, b):
    return lax.dot_general(a, b, (((1,), (1,)), ((), ())), preferred_element_type=F32)


def each(start, stop, unroll=1):
    def run(f):
        def step(i, carry):
            f(i)
            return carry

        lax.fori_loop(start, stop, step, 0, unroll=unroll)

    return run


def kernel(
    tab, pj, up, ow, tw,
    lo_out, gp_out, wg_out,
    pjv, upv, owv, twv,
    p_f, p_q, f_t, q_t, u_t, g_t, kv,
    part, outg, arr, rep, retd,
    run_t, run_s, run_k, run_v,
    s_a, s_kv, s_f, s_m, r_a, r_kv, r_f, r_m,
    wg_acc, wg_p, wx_r, wz_p, wz_r,
    ld, fs, fr, qs, qr, rs, rr, ls, lr, bs, br, ps, pr, es, er,
    as_, ar, ks, kr, hs, hr, ms, mr, xs, xr, zs, zr,
):
    s = lax.axis_index("seq")
    h = lax.axis_index("head")
    z = s // NX
    x = s % NX
    sib = h + 1 - 2 * (h % 2)
    right, left = (h + 2) % HEADS, (h + HEADS - 2) % HEADS
    my_rows = pl.ds(pl.multiple_of(h * HS, 16), HS)

    def remote(src, dst, send, recv, axis, peer):
        return pltpu.make_async_remote_copy(
            src_ref=src, dst_ref=dst, send_sem=send, recv_sem=recv,
            device_id={axis: peer}, device_id_type=MESH,
        )

    def head_copy(src, dst, send, recv):
        def at(d):
            peer = (h + d) % HEADS
            return remote(src.at[peer], dst.at[h], send.at[d], recv.at[d], "head", peer)

        return at

    def seq_copy(src, dst, send, recv):
        def at(d):
            peer = (s + d) % SHARDS
            return remote(
                src.at[pl.ds(peer * CAP, CAP)], dst.at[pl.ds(s * CAP, CAP)],
                send.at[d], recv.at[d], "seq", peer,
            )

        return at

    c_f = head_copy(p_f, f_t, fs, fr)
    c_q = head_copy(p_q, q_t, qs, qr)
    c_a = head_copy(s_a, r_a, as_, ar)
    c_kv = head_copy(s_kv, r_kv, ks, kr)
    c_df = head_copy(s_f, r_f, hs, hr)
    c_m = head_copy(s_m, r_m, ms, mr)
    c_p = seq_copy(outg, arr, ps, pr)
    c_e = seq_copy(rep, retd, es, er)

    def start_all(copy, n):
        each(1, n)(lambda d: copy(d).start())

    def recv_all(copy, n):
        each(1, n)(lambda d: copy(d).wait_recv())

    def send_all(copy, n):
        each(1, n)(lambda d: copy(d).wait_send())

    half = D // 2
    parts_right = [pl.ds(0, D)] * 3 + [pl.ds(0, half)]
    parts_left = [pl.ds(0, D)] * 3 + [pl.ds(half, half)]

    def ring_right(i):
        ref = u_t.at[(h + HEADS - 2 * i) % HEADS, parts_right[i]]
        return remote(ref, ref, rs.at[i], rr.at[i], "head", right)

    def ring_left(i):
        ref = u_t.at[(h + 2 * i) % HEADS, parts_left[i]]
        return remote(ref, ref, ls.at[i], lr.at[i], "head", left)

    def to_sib(k):
        ref = u_t.at[(h + 2 * k) % HEADS]
        return remote(ref, ref, bs.at[k], br.at[k], "head", sib)

    l_up = pltpu.make_async_copy(up, upv, ld.at[0])
    l_pj = pltpu.make_async_copy(pj, pjv, ld.at[1])
    l_tw = pltpu.make_async_copy(tw, twv, ld.at[2])
    l_ow = pltpu.make_async_copy(ow, owv, ld.at[3])
    for load in (l_up, l_pj, l_tw, l_ow):
        load.start()
    barrier = pltpu.get_barrier_semaphore()

    @each(1, HEADS)
    def _(d):
        pl.semaphore_signal(
            barrier, inc=1, device_id={"head": (h + d) % HEADS}, device_id_type=MESH
        )

    @each(1, SHARDS)
    def _(d):
        pl.semaphore_signal(
            barrier, inc=1, device_id={"seq": (s + d) % SHARDS}, device_id_type=MESH
        )

    run_t[SLOTS] = jnp.zeros((HS, BLOCK), F32)
    run_s[TILES] = jnp.zeros((HS, BLOCK), F32)
    run_k[QB * KMAX] = jnp.zeros((HS, BLOCK), F32)
    run_v[QB * KMAX] = jnp.zeros((HS, BLOCK), F32)

    l_up.wait()
    for i in range(2):
        u_t[h, half * i : half * (i + 1)] = upv[:, half * i : half * (i + 1)].T
    l_pj.wait()
    for i in range(HEADS // 2):
        pair = pjv[:, 8 * HS * i : 8 * HS * (i + 1)].T
        for k in range(2):
            p_q[2 * i + k] = pair[4 * HS * k : 4 * HS * k + 3 * HS]
            p_f[2 * i + k] = pair[4 * HS * k + 3 * HS : 4 * HS * (k + 1)]
    f_t[h] = p_f[h]
    q_t[h] = p_q[h]
    pl.semaphore_wait(barrier, HEADS + SHARDS - 2)

    start_all(c_f, HEADS)
    ring_right(0).start()
    ring_left(0).start()
    to_sib(0).start()
    start_all(c_q, HEADS)

    def ring_step(i):
        ring_right(i - 1).wait_recv()
        if i < 4:
            ring_right(i).start()
            to_sib(8 - i).start()
        ring_left(i - 1).wait_recv()
        if i < 4:
            ring_left(i).start()
            to_sib(i).start()
        else:
            to_sib(4).start()

    recv_all(c_f, HEADS)
    l_tw.wait()

    @each(0, TILES, 8)
    def _(t):
        part[t] = nt(f_t[tab[T_SRC + t]], twv[t]).astype(BF16)

    @each(0, SLOTS, 8)
    def _(p):
        outg[p] = part[tab[T_TILE_OF + p]]

    start_all(c_p, SHARDS)
    arr[pl.ds(s * CAP, CAP)] = outg[pl.ds(s * CAP, CAP)]
    ring_step(1)
    ring_step(2)
    ring_step(3)
    ring_step(4)
    each(0, 8)(lambda k: to_sib(k).wait_recv())

    @each(0, SLOTS, 8)
    def _(p):
        rep[p] = u_t[tab[T_REPLY + p], my_rows]

    start_all(c_e, SHARDS)
    retd[pl.ds(s * CAP, CAP)] = rep[pl.ds(s * CAP, CAP)]

    l_ow.wait()

    @each(0, QB, 2)
    def _(b):
        g_t[b] = nn(owv[my_rows], u_t[b]).astype(BF16)

    recv_all(c_q, HEADS)

    @each(0, QB, 2)
    def _(b):
        kv[b] = q_t[b, HS:].T

    scale = HS ** (-0.5)
    pad = jnp.zeros((HS, BLOCK), BF16)

    def attend(i):
        r = (h + 1 + i) % QB
        q = q_t[r, :HS]
        g = g_t[r]
        blocks = [tab[T_KEY + KMAX * i + j] for j in range(KMAX)]
        count = tab[T_COUNT + i]
        qg = jnp.concatenate(
            [jnp.concatenate([q, pad], axis=1), jnp.concatenate([pad, g], axis=1)], axis=0
        )
        both = [nn(kv[blocks[j]], qg) for j in range(KMAX)]
        scores = [
            both[j][:, :BLOCK] * scale + jnp.where(j < count, 0.0, -jnp.inf).astype(F32)
            for j in range(KMAX)
        ]
        grad_prob = [both[j][:, BLOCK:] for j in range(KMAX)]
        top = functools.reduce(
            jnp.maximum, [jnp.max(sc, axis=0, keepdims=True) for sc in scores]
        )
        expo = [jnp.exp(sc - top) for sc in scores]
        total = sum(jnp.sum(e, axis=0, keepdims=True) for e in expo)
        inverse = 1.0 / total
        prob = [e * inverse for e in expo]
        delta = sum(
            jnp.sum(a * b, axis=0, keepdims=True) for a, b in zip(prob, grad_prob)
        )
        prob_b = jnp.concatenate([a.astype(BF16) for a in prob], axis=0)
        dscore = jnp.concatenate(
            [(a * (b - delta) * scale).astype(BF16) for a, b in zip(prob, grad_prob)], axis=0
        )
        keys_t = jnp.concatenate([q_t[b, HS : 2 * HS] for b in blocks], axis=1)
        values_t = jnp.concatenate([q_t[b, 2 * HS :] for b in blocks], axis=1)
        s_a[r, :HS] = nn(values_t, prob_b).astype(BF16)
        s_a[r, HS:] = nn(keys_t, dscore).astype(BF16)
        term_k = nt(q, dscore)
        term_v = nt(g, prob_b)
        for j in range(KMAX):
            before = tab[T_PREV_KEY + KMAX * i + j]
            lanes = slice(BLOCK * j, BLOCK * (j + 1))
            run_k[KMAX * i + j] = term_k[:, lanes] + run_k[before]
            run_v[KMAX * i + j] = term_v[:, lanes] + run_v[before]

    @each(0, QB - 1)
    def _(i):
        attend(i)
        c_a(i + 1).start()

    attend(QB - 1)
    r_a[h] = s_a[h]

    @each(1, HEADS)
    def _(d):
        b = (h + d) % HEADS
        last = tab[T_LAST_KEY + b]
        s_kv[b, :HS] = run_k[last].astype(BF16)
        s_kv[b, HS:] = run_v[last].astype(BF16)
        c_kv(d).start()

    last_own = tab[T_LAST_KEY + h]
    r_kv[h, :HS] = run_k[last_own].astype(BF16)
    r_kv[h, HS:] = run_v[last_own].astype(BF16)

    wg_acc[...] = nt(u_t[0], s_a[0, :HS])

    @each(1, QB)
    def _(b):
        wg_acc[...] += nt(u_t[b], s_a[b, :HS])

    columns = D // SHARDS
    for n in range(SHARDS):
        wg_p[(n % NX) * NZ + n // NX] = wg_acc[columns * n : columns * (n + 1)]

    def c_x(d):
        to = (x + d) % NX
        return remote(
            wg_p.at[pl.ds(to * NZ, NZ)], wx_r.at[x], xs.at[d], xr.at[d], "seq", z * NX + to
        )

    def c_z(d):
        to = (z + d) % NZ
        return remote(wz_p.at[to], wz_r.at[z], zs.at[d], zr.at[d], "seq", to * NX + x)

    start_all(c_x, NX)
    wx_r[x] = wg_p[pl.ds(x * NZ, NZ)]

    recv_all(c_p, SHARDS)

    @each(0, SLOTS, 8)
    def _(p):
        run_t[p] = arr[p].astype(F32) + run_t[tab[T_PREV_TGT + p]]

    @each(1, HEADS)
    def _(d):
        b = (h + d) % HEADS
        s_m[b] = run_t[tab[T_LAST_TGT + b]].astype(BF16)
        c_m(d).start()

    r_m[h] = run_t[tab[T_LAST_TGT + h]].astype(BF16)

    recv_all(c_x, NX)
    wz_p[...] = wx_r[0] + wx_r[1] + wx_r[2] + wx_r[3]
    start_all(c_z, NZ)
    wz_r[z] = wz_p[z]

    recv_all(c_e, SHARDS)

    @each(0, TILES, 8)
    def _(t):
        run_s[t] = nn(retd[tab[T_SLOT_OF + t]], twv[t])

    @each(0, TILES, 8)
    def _(t):
        run_s[t] = run_s[t] + run_s[tab[T_PREV_SRC + t]]

    @each(1, HEADS)
    def _(d):
        b = (h + d) % HEADS
        s_f[b] = run_s[tab[T_LAST_SRC + b]].astype(BF16)
        c_df(d).start()

    r_f[h] = run_s[tab[T_LAST_SRC + h]].astype(BF16)

    recv_all(c_z, NZ)
    total = wz_r[0]
    for n in range(1, NZ):
        total = total + wz_r[n]
    wg_out[...] = (total * (1.0 / math.sqrt(SHARDS * QB * BLOCK))).T

    recv_all(c_a, HEADS)
    recv_all(c_m, HEADS)
    per = HEADS // 2
    acc = jnp.zeros((BLOCK, D), F32)
    for i in range(2):
        wide = jnp.concatenate([r_a[per * i + k, :HS] for k in range(per)], axis=0).T
        acc = acc + nn(wide, owv[half * i : half * (i + 1)])
    mixed = [
        jnp.concatenate([r_m[per * i + k] for k in range(per)], axis=0).T for i in range(2)
    ]
    lo_out[...] = (acc + jnp.concatenate(mixed, axis=1).astype(F32)).astype(BF16)
    recv_all(c_kv, HEADS)
    recv_all(c_df, HEADS)
    for i in range(HEADS // 2):
        rows = []
        for n in (2 * i, 2 * i + 1):
            rows += [r_a[n, HS:], r_kv[n], r_f[n]]
        gp_out[:, 8 * HS * i : 8 * HS * (i + 1)] = jnp.concatenate(rows, axis=0).T

    for copy in (c_f, c_q, c_a, c_kv, c_df, c_m):
        send_all(copy, HEADS)
    send_all(c_p, SHARDS)
    send_all(c_e, SHARDS)
    send_all(c_x, NX)
    send_all(c_z, NZ)
    for i in range(4):
        ring_right(i).wait_send()
        ring_left(i).wait_send()
    each(0, 8)(lambda k: to_sib(k).wait_send())


def last_before(same):
    n = same.shape[-1]
    return jnp.max(jnp.where(same, jnp.arange(n, dtype=jnp.int32), -1), axis=-1)


def earlier(n):
    r = jnp.arange(n, dtype=jnp.int32)
    return r[None, :] < r[:, None]


def tables(tile_owner, source_block, target_block, key_blocks, key_count):
    s = lax.axis_index("seq")
    h = lax.axis_index("head")
    blocks = jnp.arange(QB, dtype=jnp.int32)
    owners = tile_owner.reshape(SHARDS, TILES)
    targets = target_block.reshape(SHARDS, TILES)
    mine = lax.dynamic_index_in_dim(owners, s, 0, keepdims=False)
    src = lax.dynamic_slice_in_dim(source_block, s * TILES, TILES, 0)

    def chained(labels, none):
        prev = last_before((labels[:, None] == labels[None, :]) & earlier(labels.shape[0]))
        last = last_before(blocks[:, None] == labels[None, :])
        return jnp.where(prev < 0, none, prev), jnp.where(last < 0, none, last)

    rank = jnp.sum(((mine[:, None] == mine[None, :]) & earlier(TILES)).astype(jnp.int32), axis=1)
    slot_of = mine * CAP + rank
    slots = jnp.arange(SLOTS, dtype=jnp.int32)
    tile_of = jnp.maximum(last_before(slots[:, None] == slot_of[None, :]), 0)
    prev_src, last_src = chained(src, TILES)
    to_me = owners == s
    rank_in = jnp.sum((to_me[:, None, :] & earlier(TILES)[None]).astype(jnp.int32), axis=2)
    held = to_me[:, None, :] & (
        rank_in[:, None, :] == jnp.arange(CAP, dtype=jnp.int32)[None, :, None]
    )
    target = jnp.max(jnp.where(held, targets[:, None, :], -1), axis=2).reshape(SLOTS)
    prev_tgt, last_tgt = chained(target, SLOTS)
    order = (h + 1 + blocks) % QB
    keys = key_blocks[order].reshape(QB * KMAX)
    prev_key, last_key = chained(keys, QB * KMAX)
    return jnp.concatenate(
        [
            tile_of, src, slot_of, prev_src, last_src, jnp.maximum(target, 0), prev_tgt, last_tgt,
            keys, key_count[order], prev_key, last_key,
        ]
    )


def body(
    projected, upstream, out_weight, tile_weights, tile_owner,
    source_block, target_block, key_blocks, key_count,
):
    tab = tables(tile_owner, source_block, target_block, key_blocks, key_count)
    any_space = pl.BlockSpec(memory_space=pl.ANY)
    vmem = pl.BlockSpec(memory_space=pltpu.VMEM)

    def buf(*shape, dtype=BF16):
        return pltpu.VMEM(shape, dtype)

    def sems(n):
        return pltpu.SemaphoreType.DMA((n,))

    tiles = (HS, BLOCK)
    return pl.pallas_call(
        kernel,
        out_shape=(
            jax.ShapeDtypeStruct((BLOCK, D), BF16),
            jax.ShapeDtypeStruct((BLOCK, 4 * D), BF16),
            jax.ShapeDtypeStruct((HS, D // SHARDS), F32),
        ),
        in_specs=[pl.BlockSpec(memory_space=pltpu.SMEM)] + [any_space] * 4,
        out_specs=(vmem, vmem, vmem),
        scratch_shapes=[
            buf(BLOCK, 4 * D), buf(BLOCK, D), buf(D, D), buf(TILES, BLOCK, BLOCK),
            buf(HEADS, *tiles), buf(HEADS, 3 * HS, BLOCK),
            buf(HEADS, *tiles), buf(HEADS, 3 * HS, BLOCK),
            buf(QB, D, BLOCK), buf(QB, *tiles), buf(QB, BLOCK, 2 * HS),
            buf(TILES, *tiles), buf(SLOTS, *tiles), buf(SLOTS, *tiles),
            buf(SLOTS, *tiles), buf(SLOTS, *tiles),
            buf(SLOTS + 1, *tiles, dtype=F32), buf(TILES + 1, *tiles, dtype=F32),
            buf(QB * KMAX + 1, *tiles, dtype=F32), buf(QB * KMAX + 1, *tiles, dtype=F32),
            buf(HEADS, 2 * HS, BLOCK), buf(HEADS, 2 * HS, BLOCK),
            buf(HEADS, *tiles), buf(HEADS, *tiles),
            buf(HEADS, 2 * HS, BLOCK), buf(HEADS, 2 * HS, BLOCK),
            buf(HEADS, *tiles), buf(HEADS, *tiles),
            buf(D, HS, dtype=F32), buf(SHARDS, D // SHARDS, HS, dtype=F32),
            buf(NX, NZ, D // SHARDS, HS, dtype=F32),
            buf(NZ, D // SHARDS, HS, dtype=F32), buf(NZ, D // SHARDS, HS, dtype=F32),
            sems(4), sems(HEADS), sems(HEADS), sems(HEADS), sems(HEADS),
            sems(4), sems(4), sems(4), sems(4), sems(8), sems(8),
            sems(SHARDS), sems(SHARDS), sems(SHARDS), sems(SHARDS),
            sems(HEADS), sems(HEADS), sems(HEADS), sems(HEADS),
            sems(HEADS), sems(HEADS), sems(HEADS), sems(HEADS),
            sems(NX), sems(NX), sems(NZ), sems(NZ),
        ],
        compiler_params=pltpu.CompilerParams(
            collective_id=0, has_side_effects=True, vmem_limit_bytes=48 << 20
        ),
    )(tab, projected, upstream, out_weight, tile_weights)


def solution(mesh):
    in_specs = (
        P(("seq", "head"), None), P(("seq", "head"), None), P(), P("seq", None, None),
        P(), P(), P(), P("seq", None), P("seq"),
    )
    out_specs = (P(("seq", "head"), None), P(("seq", "head"), None), P("head", "seq"))
    return jax.shard_map(body, mesh=mesh, in_specs=in_specs, out_specs=out_specs, check_vma=False)
```

time: 530 us -> 111 us (0.21)
  waiting for transfers between devices: 327 us -> 0 us
  Pallas kernels: 0 us -> 96.2 us
  local copies, waits for them, and re-layouts: 90.7 us -> 10.9 us
  matrix products: 42.4 us -> 0 us
  starting transfers between devices: 41.8 us -> 0 us
  between operations: 14.6 us -> 0.78 us
    unnamed x2 -> x0, waiting for transfers between devices: 274 us -> none
    pallas_call x0 -> x1, Pallas kernels: none -> 96.2 us  [body(): pl.pallas_call(kernel, out_shape=(jax.ShapeDtypeStruct((BLOCK, D), BF16),...]
    all_to_all x6 -> x0, waiting for transfers between devices: 52.8 us -> none  [the longest x1 15 us: body(): lax.all_to_all(projected, 'head', split_axis=1, concat_axis=0, tiled=True)]
    dot_general x44 -> x0, matrix products: 42.4 us -> none  [the longest x4 10.4 us: advance(): jnp.einsum('gjb,gjkhd->bkhd', onehot_part, value_terms, precision=finest)]
    all_to_all x6 -> x0, starting transfers between devices: 41.5 us -> none  [the longest x1 11.5 us: body(): lax.all_to_all(replies, 'seq', split_axis=0, concat_axis=0, tiled=True)]
    reshape x10 -> x3, local copies, waits for them, and re-layouts: 24.8 us -> 0.27 us  [the longest x1 0.11 us: tables(): jnp.max(jnp.where(held, targets[:, None, :], -1), axis=2).reshape(SLOTS)]
    another operation x11 -> x0, local copies, waits for them, and re-layouts: 10.8 us -> none  [the longest x5 4.02 us: body(): jnp.stack([grad_query.reshape(heads_shape), grad_key.reshape(heads_shape)...]
    dynamic_slice x17 -> x1, local copies, waits for them, and re-layouts: 10.6 us -> 0.78 us  [tables(): src = lax.dynamic_slice_in_dim(source_block, s * TILES, TILES, 0)]
  transfers between devices with their start and end apart: 7 -> 0, of which waited for: 6 -> 0; matrix products, arithmetic and copies ran while one was open for 23% -> 0% of each run, Pallas kernels for 0% -> 0%
where the time goes in v1:
time: 111 us
  Pallas kernels  96.2 us (87%)
  local copies, waits for them, and re-layouts  10.9 us (10%)
  other arithmetic  2.75 us (2%)
    pallas_call x1, Pallas kernels, body(): pl.pallas_call(kernel, out_shape=(jax.ShapeDtypeStruct((BLOCK, D), BF16),...  96.2 us
    unnamed x13, local copies, waits for them, and re-layouts  7.06 us

profile of v1, /device:TPU:1, one launch (start us, length us, event | category | flops | bytes accessed | tf_op | source)
XLA Modules:
  0.0 110.7 jit_solution(1854304823035191926)
XLA Ops:
  0.6 0.0 copy-start
  0.7 0.8 dynamic_slice.8
  1.4 0.1 select_reduce_fusion.7
  1.6 0.2 select_reduce_fusion.3
  1.8 0.0 copy-done
  1.8 0.7 gather_fusion.1
  2.5 0.7 reduce
  3.2 0.1 reshape.92
  3.3 0.2 convert_reduce_fusion.1
  3.5 0.1 select_reduce_fusion.4
  3.6 0.8 copy.17
  4.4 0.6 gather_fusion
  4.9 0.1 reshape.94
  5.0 0.1 select_reduce_fusion.5
  5.1 0.2 select_reduce_fusion.2
  5.3 0.6 convert_reduce_fusion
  6.0 0.8 broadcast_in_dim.127
  6.7 0.2 select_reduce_fusion.1
  6.9 0.1 copy.16
  7.0 0.1 reshape.93
  7.1 0.2 select_reduce_fusion
  7.3 0.1 select_reduce_fusion.6
  7.4 0.1 concatenate.3.tab
  7.5 0.0 copy-start.1
  7.5 1.4 %copy-done.1 = bf16[48,128,128]{2,1,0:T(8,128)(2,1)S(1)} copy-done((bf16[48,128,128]{2,1,0:T(8,128)(2,1)S(1)}, bf16[48,128,128]{2,1,0:T(8,128)(2,1)}, u32[]{:S(2)}) %copy-start.1) | copy-done | bytes 1572888
  8.9 0.0 copy-start.2
  8.9 1.3 %copy-done.2 = bf16[768,768]{1,0:T(8,128)(2,1)S(1)} copy-done((bf16[768,768]{1,0:T(8,128)(2,1)S(1)}, bf16[768,768]{1,0:T(8,128)(2,1)}, u32[]{:S(2)}) %copy-start.2) | copy-done | bytes 1179672
  10.2 0.0 copy-start.3
  10.2 1.1 %copy-done.3 = bf16[128,3072]{1,0:T(8,128)(2,1)S(1)} copy-done((bf16[128,3072]{1,0:T(8,128)(2,1)S(1)}, bf16[128,3072]{1,0:T(8,128)(2,1)}, u32[]{:S(2)}) %copy-start.3) | copy-done | bytes 786456
  11.3 0.0 copy-start.4
  11.3 0.9 copy-done.4
  12.2 96.2 %shard_map.112 = (bf16[128,768]{1,0:T(8,128)(2,1)S(1)}, bf16[128,3072]{1,0:T(8,128)(2,1)S(1)}, f32[48,24]{1,0:T(8,128)S(1)}) custom-call(s32[624]{0:T(1024)S(1)} %concatenate.3.tab, bf16[128,3072]{1,0:T(8,128)(2,1)S(1)} %copy-done.3, bf16[128,768]{1,0:T(8,128)(2,1)S(1)} %copy-done.4, bf16[768,768]{1,0:T(8,128)(2,1)S(1)} %copy-done.2, ...), custom_call_target="tpu_custom_call" | custom-call | tf_op jit(solution)/shard_map/pallas_call | solution.py:455
  108.4 0.7 copy.18
  109.1 0.7 copy.21
  109.8 0.9 copy.22
  (12 shorter events, 0.1 us)
Async XLA Ops:
  0.6 1.1 %copy-start = (s32[16]{0:T(128)S(1)}, s32[16]{0:T(128)}, u32[]{:S(2)}) copy-start(s32[16]{0:T(128)} %param.17) | copy-start | bytes 196
  7.5 1.4 %copy-start.1 = (bf16[48,128,128]{2,1,0:T(8,128)(2,1)S(1)}, bf16[48,128,128]{2,1,0:T(8,128)(2,1)}, u32[]{:S(2)}) copy-start(bf16[48,128,128]{2,1,0:T(8,128)(2,1)} %tw.1) | copy-start | bytes 4718596
  8.9 1.3 %copy-start.2 = (bf16[768,768]{1,0:T(8,128)(2,1)S(1)}, bf16[768,768]{1,0:T(8,128)(2,1)}, u32[]{:S(2)}) copy-start(bf16[768,768]{1,0:T(8,128)(2,1)} %ow.1) | copy-start | bytes 3538948
  10.2 1.1 %copy-start.3 = (bf16[128,3072]{1,0:T(8,128)(2,1)S(1)}, bf16[128,3072]{1,0:T(8,128)(2,1)}, u32[]{:S(2)}) copy-start(bf16[128,3072]{1,0:T(8,128)(2,1)} %pj.1) | copy-start | bytes 2359300
  11.3 0.9 copy-start.4

commit v2 on v1

v2 whole, which is shorter than its diff:
```python
import functools
import math

import jax
import jax.numpy as jnp
from jax import lax
from jax.experimental import pallas as pl
from jax.experimental.pallas import tpu as pltpu
from jax.sharding import PartitionSpec as P

MESH = pl.DeviceIdType.MESH
HEADS = 16
BLOCK = 128
CAP = 3
HS = 48
D = 768
QB = 16
KMAX = 4
TILES = 48
SHARDS = 32
SLOTS = SHARDS * CAP
NX = 4
NZ = 8
F32 = jnp.float32
BF16 = jnp.bfloat16

SLOT_OF, PREV_SRC, LAST_SRC, PREV_TGT, LAST_TGT, PREV_KEY, LAST_KEY = range(7)


def nn(a, b):
    return lax.dot_general(a, b, (((1,), (0,)), ((), ())), preferred_element_type=F32)


def nt(a, b):
    return lax.dot_general(a, b, (((1,), (1,)), ((), ())), preferred_element_type=F32)


def each(start, stop, unroll=1):
    def run(f):
        def step(i, carry):
            f(i)
            return carry

        lax.fori_loop(start, stop, step, 0, unroll=unroll)

    return run


def kernel(
    own_in, sources_in, targets_in, keys_in, counts_in, pj, up, ow, tw,
    lo_out, q_out, r_kv, r_f, wg_out,
    own, sources, targets, keys, counts, lo_v, wg_v,
    own_m, slots_v, slots, chains_v, chains,
    pjv, upv, owv, twv,
    p_f, p_q, f_t, q_t, u_t, g_t, kv,
    part, outg, arr, rep, retd,
    run_t, run_s, run_k, run_v,
    s_a, s_kv, s_f, s_m, r_a, r_m,
    wg_acc, wg_p, wx_r, wz_p, wz_r,
    ld, tb, out, fs, fr, qs, qr, rs, rr, ls, lr, bs, br, ps, pr, es, er,
    as_, ar, ks, kr, hs, hr, ms, mr, xs, xr, zs, zr,
):
    s = lax.axis_index("seq")
    h = lax.axis_index("head")
    z = s // NX
    x = s % NX
    sib = h + 1 - 2 * (h % 2)
    right, left = (h + 2) % HEADS, (h + HEADS - 2) % HEADS
    my_rows = pl.ds(pl.multiple_of(h * HS, 16), HS)

    def remote(src, dst, send, recv, axis, peer):
        return pltpu.make_async_remote_copy(
            src_ref=src, dst_ref=dst, send_sem=send, recv_sem=recv,
            device_id={axis: peer}, device_id_type=MESH,
        )

    def head_copy(src, dst, send, recv):
        def at(d):
            peer = (h + d) % HEADS
            return remote(src.at[peer], dst.at[h], send.at[d], recv.at[d], "head", peer)

        return at

    def seq_copy(src, dst, send, recv):
        def at(d):
            peer = (s + d) % SHARDS
            return remote(
                src.at[pl.ds(peer * CAP, CAP)], dst.at[pl.ds(s * CAP, CAP)],
                send.at[d], recv.at[d], "seq", peer,
            )

        return at

    c_f = head_copy(p_f, f_t, fs, fr)
    c_q = head_copy(p_q, q_t, qs, qr)
    c_a = head_copy(s_a, r_a, as_, ar)
    c_kv = head_copy(s_kv, r_kv, ks, kr)
    c_df = head_copy(s_f, r_f, hs, hr)
    c_m = head_copy(s_m, r_m, ms, mr)
    c_p = seq_copy(outg, arr, ps, pr)
    c_e = seq_copy(rep, retd, es, er)

    def start_all(copy, n):
        each(1, n)(lambda d: copy(d).start())

    def recv_all(copy, n):
        each(1, n)(lambda d: copy(d).wait_recv())

    def send_all(copy, n):
        each(1, n)(lambda d: copy(d).wait_send())

    half = D // 2
    parts_right = [pl.ds(0, D)] * 3 + [pl.ds(0, half)]
    parts_left = [pl.ds(0, D)] * 3 + [pl.ds(half, half)]

    def ring_right(i):
        ref = u_t.at[(h + HEADS - 2 * i) % HEADS, parts_right[i]]
        return remote(ref, ref, rs.at[i], rr.at[i], "head", right)

    def ring_left(i):
        ref = u_t.at[(h + 2 * i) % HEADS, parts_left[i]]
        return remote(ref, ref, ls.at[i], lr.at[i], "head", left)

    def to_sib(k):
        ref = u_t.at[(h + 2 * k) % HEADS]
        return remote(ref, ref, bs.at[k], br.at[k], "head", sib)

    l_up = pltpu.make_async_copy(up, upv, ld.at[0])
    l_pj = pltpu.make_async_copy(pj, pjv, ld.at[1])
    l_tw = pltpu.make_async_copy(tw, twv, ld.at[2])
    l_ow = pltpu.make_async_copy(ow, owv, ld.at[3])
    small = (
        (own_in, own), (sources_in, sources), (targets_in, targets), (keys_in, keys),
        (counts_in, counts),
    )
    l_small = [pltpu.make_async_copy(a, b, ld.at[4 + n]) for n, (a, b) in enumerate(small)]
    l_pj.start()
    l_up.start()
    barrier = pltpu.get_barrier_semaphore()
    for d in range(1, HEADS):
        pl.semaphore_signal(
            barrier, inc=1, device_id={"head": (h + d) % HEADS}, device_id_type=MESH
        )
    for d in range(1, SHARDS):
        pl.semaphore_signal(
            barrier, inc=1, device_id={"seq": (s + d) % SHARDS}, device_id_type=MESH
        )
    for load in (*l_small, l_tw, l_ow):
        load.start()
    l_pj.wait()
    for i in range(HEADS // 2):
        pair = pjv[:, 8 * HS * i : 8 * HS * (i + 1)].T
        for k in range(2):
            p_q[2 * i + k] = pair[4 * HS * k : 4 * HS * k + 3 * HS]
            p_f[2 * i + k] = pair[4 * HS * k + 3 * HS : 4 * HS * (k + 1)]
    pl.semaphore_wait(barrier, HEADS + SHARDS - 2)

    start_all(c_f, HEADS)
    f_t[h] = p_f[h]
    q_t[h] = p_q[h]
    l_up.wait()
    for i in range(2):
        u_t[h, half * i : half * (i + 1)] = upv[:, half * i : half * (i + 1)].T
    run_t[SLOTS] = jnp.zeros((HS, BLOCK), F32)
    run_s[TILES] = jnp.zeros((HS, BLOCK), F32)
    run_k[QB * KMAX] = jnp.zeros((HS, BLOCK), F32)
    run_v[QB * KMAX] = jnp.zeros((HS, BLOCK), F32)

    def ring_step(i):
        ring_right(i - 1).wait_recv()
        if i < 4:
            ring_right(i).start()
            to_sib(8 - i).start()
        ring_left(i - 1).wait_recv()
        if i < 4:
            ring_left(i).start()
            to_sib(i).start()
        else:
            to_sib(4).start()

    for load in l_small:
        load.wait()
    for n in range(SHARDS):
        own_m[n : n + 1, :TILES] = own[:, TILES * n : TILES * (n + 1)]
    lane = lax.broadcasted_iota(jnp.int32, (SHARDS, BLOCK), 1)
    row = lax.broadcasted_iota(jnp.int32, (SHARDS, BLOCK), 0)
    lane1 = lax.broadcasted_iota(jnp.int32, (1, BLOCK), 1)

    def first_three(same):
        found = []
        for k in range(CAP):
            later = same & (lane > found[-1]) if k else same
            found.append(jnp.min(jnp.where(later, lane, 999), axis=1, keepdims=True))
        return found

    def in_lanes(found, none):
        listed = jnp.where(lane == 0, found[0], jnp.where(lane == 1, found[1], found[2]))
        return jnp.where(listed == 999, none, listed)

    mine = own_m[pl.ds(s, 1), :]
    going = first_three((mine == row) & (lane < TILES))
    coming = first_three((own_m[...] == s) & (lane < TILES))
    slots_v[:SHARDS] = in_lanes(going, 0)
    slots_v[SHARDS:] = in_lanes(coming, -1)
    l_slots = pltpu.make_async_copy(slots_v, slots, tb.at[0])
    l_slots.start()
    rank = jnp.where(lane == going[1], 1, jnp.where(lane == going[2], 2, 0))
    slot_of = CAP * jnp.where(lane1 < TILES, mine, 0) + jnp.max(rank, axis=0, keepdims=True)
    chains_v[SLOT_OF : SLOT_OF + 1] = slot_of

    def slot_target(n, k):
        tile = slots[SHARDS + n, k]
        return tile, targets[TILES * n + jnp.maximum(tile, 0)]

    def chain(outer, inner, label, none, prev_row, last_row):
        def gather(i, labels):
            for j in range(inner):
                labels = jnp.where(lane1 == inner * i + j, label(i, j), labels)
            return labels

        labels = lax.fori_loop(0, outer, gather, jnp.full((1, BLOCK), -2, jnp.int32))

        def link(i, carry):
            prev, last = carry
            for j in range(inner):
                at, here = inner * i + j, label(i, j)
                prev = jnp.where((labels == here) & (lane1 > at), at, prev)
                last = jnp.where(lane1 == here, at, last)
            return prev, last

        empty = jnp.full((1, BLOCK), none, jnp.int32)
        prev, last = lax.fori_loop(0, outer, link, (empty, empty))
        chains_v[prev_row : prev_row + 1] = prev
        chains_v[last_row : last_row + 1] = last

    def source(i, j):
        return sources[TILES * s + 4 * i + j]

    def target(i, j):
        tile, at = slot_target(i, j)
        return jnp.where(tile < 0, -1, at)

    def key(i, j):
        return keys[j, (h + 1 + i) % QB]

    l_slots.wait()
    recv_all(c_f, HEADS)
    ring_right(0).start()
    ring_left(0).start()
    to_sib(0).start()
    l_tw.wait()

    @each(0, TILES, 8)
    def _(t):
        part[t] = nt(f_t[sources[TILES * s + t]], twv[t]).astype(BF16)

    @each(0, SHARDS, 4)
    def _(n):
        for k in range(CAP):
            outg[CAP * n + k] = part[slots[n, k]]

    start_all(c_p, SHARDS)
    arr[pl.ds(s * CAP, CAP)] = outg[pl.ds(s * CAP, CAP)]
    chain(TILES // 4, 4, source, TILES, PREV_SRC, LAST_SRC)
    ring_step(1)
    chain(QB, KMAX, key, QB * KMAX, PREV_KEY, LAST_KEY)
    ring_step(2)
    each(1, 5)(lambda d: c_q(d).start())
    chain(SHARDS, CAP, target, SLOTS, PREV_TGT, LAST_TGT)
    l_chains = pltpu.make_async_copy(chains_v, chains, tb.at[1])
    l_chains.start()
    ring_step(3)
    each(5, 9)(lambda d: c_q(d).start())
    ring_step(4)
    each(9, HEADS)(lambda d: c_q(d).start())
    each(0, 8)(lambda k: to_sib(k).wait_recv())
    l_chains.wait()

    @each(0, SHARDS, 4)
    def _(n):
        for k in range(CAP):
            rep[CAP * n + k] = u_t[slot_target(n, k)[1], my_rows]

    start_all(c_e, SHARDS)
    retd[pl.ds(s * CAP, CAP)] = rep[pl.ds(s * CAP, CAP)]

    l_ow.wait()

    @each(0, QB, 2)
    def _(b):
        g_t[b] = nn(owv[my_rows], u_t[b]).astype(BF16)

    recv_all(c_p, SHARDS)

    @each(0, SLOTS, 8)
    def _(p):
        run_t[p] = arr[p].astype(F32) + run_t[chains[PREV_TGT, p]]

    @each(1, HEADS)
    def _(d):
        b = (h + d) % HEADS
        s_m[b] = run_t[chains[LAST_TGT, b]].astype(BF16)
        c_m(d).start()

    r_m[h] = run_t[chains[LAST_TGT, h]].astype(BF16)

    recv_all(c_q, HEADS)

    @each(0, QB, 2)
    def _(b):
        kv[b] = q_t[b, HS:].T

    scale = HS ** (-0.5)
    pad = jnp.zeros((HS, BLOCK), BF16)

    def attend(i):
        r = (h + 1 + i) % QB
        q = q_t[r, :HS]
        g = g_t[r]
        blocks = [keys[j, r] for j in range(KMAX)]
        count = counts[r]
        qg = jnp.concatenate(
            [jnp.concatenate([q, pad], axis=1), jnp.concatenate([pad, g], axis=1)], axis=0
        )
        both = [nn(kv[blocks[j]], qg) for j in range(KMAX)]
        scores = [
            both[j][:, :BLOCK] * scale + jnp.where(j < count, 0.0, -jnp.inf).astype(F32)
            for j in range(KMAX)
        ]
        grad_prob = [both[j][:, BLOCK:] for j in range(KMAX)]
        top = functools.reduce(
            jnp.maximum, [jnp.max(sc, axis=0, keepdims=True) for sc in scores]
        )
        expo = [jnp.exp(sc - top) for sc in scores]
        total = sum(jnp.sum(e, axis=0, keepdims=True) for e in expo)
        inverse = 1.0 / total
        prob = [e * inverse for e in expo]
        delta = sum(
            jnp.sum(a * b, axis=0, keepdims=True) for a, b in zip(prob, grad_prob)
        )
        prob_b = jnp.concatenate([a.astype(BF16) for a in prob], axis=0)
        dscore = jnp.concatenate(
            [(a * (b - delta) * scale).astype(BF16) for a, b in zip(prob, grad_prob)], axis=0
        )
        keys_t = jnp.concatenate([q_t[b, HS : 2 * HS] for b in blocks], axis=1)
        values_t = jnp.concatenate([q_t[b, 2 * HS :] for b in blocks], axis=1)
        s_a[r, :HS] = nn(values_t, prob_b).astype(BF16)
        s_a[r, HS:] = nn(keys_t, dscore).astype(BF16)
        term_k = nt(q, dscore)
        term_v = nt(g, prob_b)
        for j in range(KMAX):
            before = chains[PREV_KEY, KMAX * i + j]
            lanes = slice(BLOCK * j, BLOCK * (j + 1))
            run_k[KMAX * i + j] = term_k[:, lanes] + run_k[before]
            run_v[KMAX * i + j] = term_v[:, lanes] + run_v[before]

    @each(0, QB - 1)
    def _(i):
        attend(i)
        c_a(i + 1).start()

    attend(QB - 1)
    r_a[h] = s_a[h]

    @each(1, HEADS)
    def _(d):
        b = (h + d) % HEADS
        last = chains[LAST_KEY, b]
        s_kv[b, :HS] = run_k[last].astype(BF16)
        s_kv[b, HS:] = run_v[last].astype(BF16)
        c_kv(d).start()

    last_own = chains[LAST_KEY, h]
    s_kv[h, :HS] = run_k[last_own].astype(BF16)
    s_kv[h, HS:] = run_v[last_own].astype(BF16)
    o_kv = pltpu.make_async_copy(s_kv.at[h], r_kv.at[h], out.at[0])
    o_kv.start()

    wg_acc[...] = nt(u_t[0], s_a[0, :HS])

    @each(1, QB)
    def _(b):
        wg_acc[...] += nt(u_t[b], s_a[b, :HS])

    columns = D // SHARDS
    for n in range(SHARDS):
        wg_p[(n % NX) * NZ + n // NX] = wg_acc[columns * n : columns * (n + 1)]

    def c_x(d):
        to = (x + d) % NX
        return remote(
            wg_p.at[pl.ds(to * NZ, NZ)], wx_r.at[x], xs.at[d], xr.at[d], "seq", z * NX + to
        )

    def c_z(d):
        to = (z + d) % NZ
        return remote(wz_p.at[to], wz_r.at[z], zs.at[d], zr.at[d], "seq", to * NX + x)

    start_all(c_x, NX)
    wx_r[x] = wg_p[pl.ds(x * NZ, NZ)]

    recv_all(c_x, NX)
    wz_p[...] = wx_r[0] + wx_r[1] + wx_r[2] + wx_r[3]
    wz_r[z] = wz_p[z]

    recv_all(c_e, SHARDS)
    start_all(c_z, NZ)

    @each(0, TILES, 8)
    def _(t):
        run_s[t] = nn(retd[chains[SLOT_OF, t]], twv[t])

    @each(0, TILES, 8)
    def _(t):
        run_s[t] = run_s[t] + run_s[chains[PREV_SRC, t]]

    @each(1, HEADS)
    def _(d):
        b = (h + d) % HEADS
        s_f[b] = run_s[chains[LAST_SRC, b]].astype(BF16)
        c_df(d).start()

    s_f[h] = run_s[chains[LAST_SRC, h]].astype(BF16)
    o_f = pltpu.make_async_copy(s_f.at[h], r_f.at[h], out.at[1])
    o_f.start()

    recv_all(c_a, HEADS)
    o_q = pltpu.make_async_copy(r_a.at[:, pl.ds(HS, HS)], q_out, out.at[3])
    o_q.start()
    recv_all(c_m, HEADS)
    per = HEADS // 2
    acc = jnp.zeros((BLOCK, D), F32)
    for i in range(2):
        wide = jnp.concatenate([r_a[per * i + k, :HS] for k in range(per)], axis=0).T
        acc = acc + nn(wide, owv[half * i : half * (i + 1)])
    mixed = [
        jnp.concatenate([r_m[per * i + k] for k in range(per)], axis=0).T for i in range(2)
    ]
    lo_v[...] = (acc + jnp.concatenate(mixed, axis=1).astype(F32)).astype(BF16)
    o_lo = pltpu.make_async_copy(lo_v, lo_out, out.at[4])
    o_lo.start()
    recv_all(c_z, NZ)
    total = wz_r[0]
    for n in range(1, NZ):
        total = total + wz_r[n]
    wg_v[...] = total * (1.0 / math.sqrt(SHARDS * QB * BLOCK))
    o_wg = pltpu.make_async_copy(wg_v, wg_out, out.at[2])
    o_wg.start()

    recv_all(c_kv, HEADS)
    recv_all(c_df, HEADS)
    for copy in (o_kv, o_f, o_wg, o_q, o_lo):
        copy.wait()

    for copy in (c_f, c_q, c_a, c_kv, c_df, c_m):
        send_all(copy, HEADS)
    send_all(c_p, SHARDS)
    send_all(c_e, SHARDS)
    send_all(c_x, NX)
    send_all(c_z, NZ)
    for i in range(4):
        ring_right(i).wait_send()
        ring_left(i).wait_send()
    each(0, 8)(lambda k: to_sib(k).wait_send())


def finish(
    lo, q, kv, f, wg, lo_out, gp_out, wg_out, lo_v, q_v, kv_v, f_v, wg_v, gp_v, sem
):
    loads = [
        pltpu.make_async_copy(a, b, sem.at[n])
        for n, (a, b) in enumerate(((lo, lo_v), (wg, wg_v), (q, q_v), (kv, kv_v), (f, f_v)))
    ]
    for copy in loads:
        copy.start()
    stores = [
        pltpu.make_async_copy(a, b, sem.at[9 + n])
        for n, (a, b) in enumerate(((lo_v, lo_out), (wg_v, wg_out)))
    ]
    for copy in loads:
        copy.wait()
    for copy in stores:
        copy.start()
    wide = 8 * HS
    for i in range(HEADS // 2):
        rows = []
        for n in (2 * i, 2 * i + 1):
            rows += [q_v[n], kv_v[n], f_v[n]]
        lanes = pl.ds(wide * i, wide)
        gp_v[:, lanes] = jnp.concatenate(rows, axis=0).T
        if i % 2:
            lanes = pl.ds(wide * (i - 1), 2 * wide)
            stores.append(
                pltpu.make_async_copy(gp_v.at[:, lanes], gp_out.at[:, lanes], sem.at[5 + i // 2])
            )
            stores[-1].start()
    for copy in stores:
        copy.wait()


def body(
    projected, upstream, out_weight, tile_weights, tile_owner,
    source_block, target_block, key_blocks, key_count,
):
    any_space = pl.BlockSpec(memory_space=pl.ANY)

    def buf(*shape, dtype=BF16):
        return pltpu.VMEM(shape, dtype)

    def sems(n):
        return pltpu.SemaphoreType.DMA((n,))

    tiles = (HS, BLOCK)
    tall = jax.ShapeDtypeStruct((HEADS, *tiles), BF16)
    columns = D // SHARDS
    lo, q, kv, f, wg = pl.pallas_call(
        kernel,
        out_shape=(
            jax.ShapeDtypeStruct((BLOCK, D), BF16),
            tall,
            jax.ShapeDtypeStruct((HEADS, 2 * HS, BLOCK), BF16),
            tall,
            jax.ShapeDtypeStruct((columns, HS), F32),
        ),
        in_specs=[any_space] * 9,
        out_specs=(any_space,) * 5,
        scratch_shapes=[
            buf(1, SHARDS * TILES, dtype=jnp.int32), pltpu.SMEM((SHARDS * TILES,), jnp.int32),
            pltpu.SMEM((SHARDS * TILES,), jnp.int32), pltpu.SMEM((KMAX, QB), jnp.int32),
            pltpu.SMEM((QB,), jnp.int32), buf(BLOCK, D), buf(columns, HS, dtype=F32),
            buf(SHARDS, BLOCK, dtype=jnp.int32), buf(2 * SHARDS, BLOCK, dtype=jnp.int32),
            pltpu.SMEM((2 * SHARDS, BLOCK), jnp.int32),
            buf(8, BLOCK, dtype=jnp.int32), pltpu.SMEM((8, BLOCK), jnp.int32),
            buf(BLOCK, 4 * D), buf(BLOCK, D), buf(D, D), buf(TILES, BLOCK, BLOCK),
            buf(HEADS, *tiles), buf(HEADS, 3 * HS, BLOCK),
            buf(HEADS, *tiles), buf(HEADS, 3 * HS, BLOCK),
            buf(QB, D, BLOCK), buf(QB, *tiles), buf(QB, BLOCK, 2 * HS),
            buf(TILES, *tiles), buf(SLOTS, *tiles), buf(SLOTS, *tiles),
            buf(SLOTS, *tiles), buf(SLOTS, *tiles),
            buf(SLOTS + 1, *tiles, dtype=F32), buf(TILES + 1, *tiles, dtype=F32),
            buf(QB * KMAX + 1, *tiles, dtype=F32), buf(QB * KMAX + 1, *tiles, dtype=F32),
            buf(HEADS, 2 * HS, BLOCK), buf(HEADS, 2 * HS, BLOCK),
            buf(HEADS, *tiles), buf(HEADS, *tiles),
            buf(HEADS, 2 * HS, BLOCK), buf(HEADS, *tiles),
            buf(D, HS, dtype=F32), buf(SHARDS, D // SHARDS, HS, dtype=F32),
            buf(NX, NZ, D // SHARDS, HS, dtype=F32),
            buf(NZ, D // SHARDS, HS, dtype=F32), buf(NZ, D // SHARDS, HS, dtype=F32),
            sems(9), sems(2), sems(5), sems(HEADS), sems(HEADS), sems(HEADS), sems(HEADS),
            sems(4), sems(4), sems(4), sems(4), sems(8), sems(8),
            sems(SHARDS), sems(SHARDS), sems(SHARDS), sems(SHARDS),
            sems(HEADS), sems(HEADS), sems(HEADS), sems(HEADS),
            sems(HEADS), sems(HEADS), sems(HEADS), sems(HEADS),
            sems(NX), sems(NX), sems(NZ), sems(NZ),
        ],
        compiler_params=pltpu.CompilerParams(
            collective_id=0, has_side_effects=True, vmem_limit_bytes=61 << 20
        ),
    )(
        tile_owner.T, source_block, target_block, key_blocks.T, key_count,
        projected, upstream, out_weight, tile_weights,
    )
    layer_out, grad_projected, weight_grad = pl.pallas_call(
        finish,
        out_shape=(
            jax.ShapeDtypeStruct((BLOCK, D), BF16),
            jax.ShapeDtypeStruct((BLOCK, 4 * D), BF16),
            jax.ShapeDtypeStruct((columns, HS), F32),
        ),
        in_specs=[any_space] * 5,
        out_specs=(any_space,) * 3,
        scratch_shapes=[
            buf(BLOCK, D), buf(HEADS, *tiles), buf(HEADS, 2 * HS, BLOCK), buf(HEADS, *tiles),
            buf(columns, HS, dtype=F32), buf(BLOCK, 4 * D), sems(11),
        ],
        compiler_params=pltpu.CompilerParams(vmem_limit_bytes=61 << 20),
    )(lo, q, kv, f, wg)
    return layer_out, grad_projected, weight_grad.T


def solution(mesh):
    in_specs = (
        P(("seq", "head"), None), P(("seq", "head"), None), P(), P("seq", None, None),
        P(), P(), P(), P("seq", None), P("seq"),
    )
    out_specs = (P(("seq", "head"), None), P(("seq", "head"), None), P("head", "seq"))
    return jax.shard_map(body, mesh=mesh, in_specs=in_specs, out_specs=out_specs, check_vma=False)
```

time: 111 us -> 100 us (0.901)
  local copies, waits for them, and re-layouts: 10.9 us -> 0 us
  Pallas kernels: 96.2 us -> 99.5 us
  other arithmetic: 2.75 us -> 0 us
    unnamed x13 -> x0, local copies, waits for them, and re-layouts: 7.06 us -> none
    pallas_call x0 -> x1, Pallas kernels: none -> 2.33 us  [body(): pl.pallas_call(finish, out_shape=(jax.ShapeDtypeStruct((BLOCK, D), BF16),...]
    gather x2 -> x0, local copies, waits for them, and re-layouts: 1.22 us -> none  [the longest x1 0.66 us: tables(): key_count[order]]
    reduce_max x8 -> x0, other arithmetic: 1.15 us -> none  [the longest x7 0.99 us: last_before(): return jnp.max(jnp.where(same, jnp.arange(n, dtype=jnp.int32), -1), axis=-1)]
where the time goes in v2:
time: 100 us
  Pallas kernels  99.5 us (100%)
    pallas_call x1, Pallas kernels, body(): pl.pallas_call(kernel, out_shape=(jax.ShapeDtypeStruct((BLOCK, D), BF16),...  97.1 us
    pallas_call x1, Pallas kernels, body(): pl.pallas_call(finish, out_shape=(jax.ShapeDtypeStruct((BLOCK, D), BF16),...  2.33 us

profile of v2, /device:TPU:1, one launch (start us, length us, event | category | flops | bytes accessed | tf_op | source)
XLA Modules:
  0.0 100.1 jit_solution(13558220094281223708)
XLA Ops:
  0.6 97.1 %shard_map.112 = (bf16[128,768]{1,0:T(8,128)(2,1)}, bf16[16,48,128]{2,1,0:T(8,128)(2,1)}, bf16[16,96,128]{2,1,0:T(8,128)(2,1)}, bf16[16,48,128]{2,1,0:T(8,128)(2,1)}, f32[24,48]{1,0:T(8,128)}) custom-call(s32[1,1536]{1,0:T(1,128)} %bitcast.3, s32[1536]{0:T(1024)} %sources_in.1, s32[1536]{0:T(1024)} %targets_in.1, s32[4,16]{1,0:T(4,128)} %bitcast.4, ...), custom_call_target="tpu_custom_call" | custom-call | tf_op jit(solution)/shard_map/pallas_call | solution.py:516
  97.8 2.3 %shard_map.113 = (bf16[128,768]{1,0:T(8,128)(2,1)}, bf16[128,3072]{1,0:T(8,128)(2,1)}, f32[24,48]{1,0:T(8,128)}) custom-call(bf16[128,768]{1,0:T(8,128)(2,1)} %get-tuple-element.11.lo, bf16[16,48,128]{2,1,0:T(8,128)(2,1)} %get-tuple-element.12.q, bf16[16,96,128]{2,1,0:T(8,128)(2,1)} %get-tuple-element.13.kv, bf16[16,48,128]{2,1,0:T(8,128)(2,1)} %get-tuple-element.14.f, ...), custom_call_target="tpu_custom_call" | custom-call | tf_op jit(solution)/shard_map/pallas_call | solution.py:562

commit v3 on v2

--- a/solution.py
+++ b/solution.py
@@ -24,7 +24,8 @@
 F32 = jnp.float32
 BF16 = jnp.bfloat16
 
-SLOT_OF, PREV_SRC, LAST_SRC, PREV_TGT, LAST_TGT, PREV_KEY, LAST_KEY = range(7)
+PREV_SRC, LAST_SRC, PREV_TGT, LAST_TGT, PREV_KEY, LAST_KEY = range(6)
+FEW, MANY = 16, 32
 
 
 def nn(a, b):
@@ -48,17 +49,18 @@
 
 def kernel(
     own_in, sources_in, targets_in, keys_in, counts_in, pj, up, ow, tw,
-    lo_out, q_out, r_kv, r_f, wg_out,
+    lo_out, q_out, r_kv, r_fa, r_fb, wg_out,
     own, sources, targets, keys, counts, lo_v, wg_v,
     own_m, slots_v, slots, chains_v, chains,
     pjv, upv, owv, twv,
-    p_f, p_q, f_t, q_t, u_t, g_t, kv,
-    part, outg, arr, rep, retd,
-    run_t, run_s, run_k, run_v,
-    s_a, s_kv, s_f, s_m, r_a, r_m,
+    p_fa, p_fb, p_q, f_ta, f_tb, q_t, u_t, g_t, kv,
+    part_a, part_b, outg_a, outg_b, arr_a, arr_b, rep_a, rep_b, ret_a, ret_b,
+    run_t, run_sa, run_sb, run_k, run_v,
+    s_a, s_kv, s_fa, s_fb, s_m, r_a, r_m,
     wg_acc, wg_p, wx_r, wz_p, wz_r,
-    ld, tb, out, fs, fr, qs, qr, rs, rr, ls, lr, bs, br, ps, pr, es, er,
-    as_, ar, ks, kr, hs, hr, ms, mr, xs, xr, zs, zr,
+    ld, tb, out, fas, far, fbs, fbr, qs, qr, rs, rr, ls, lr, bs, br,
+    pas, par, pbs, pbr, eas, ear, ebs, ebr,
+    as_, ar, ks, kr, has, har, hbs, hbr, ms, mr, xs, xr, zs, zr,
 ):
     s = lax.axis_index("seq")
     h = lax.axis_index("head")
@@ -67,6 +69,8 @@
     sib = h + 1 - 2 * (h % 2)
     right, left = (h + 2) % HEADS, (h + HEADS - 2) % HEADS
     my_rows = pl.ds(pl.multiple_of(h * HS, 16), HS)
+    my_many = pl.ds(pl.multiple_of(h * HS, 16), MANY)
+    my_few = pl.ds(pl.multiple_of(h * HS + MANY, 16), FEW)
 
     def remote(src, dst, send, recv, axis, peer):
         return pltpu.make_async_remote_copy(
@@ -91,14 +95,18 @@
 
         return at
 
-    c_f = head_copy(p_f, f_t, fs, fr)
+    c_fa = head_copy(p_fa, f_ta, fas, far)
+    c_fb = head_copy(p_fb, f_tb, fbs, fbr)
     c_q = head_copy(p_q, q_t, qs, qr)
     c_a = head_copy(s_a, r_a, as_, ar)
     c_kv = head_copy(s_kv, r_kv, ks, kr)
-    c_df = head_copy(s_f, r_f, hs, hr)
+    c_dfa = head_copy(s_fa, r_fa, has, har)
+    c_dfb = head_copy(s_fb, r_fb, hbs, hbr)
     c_m = head_copy(s_m, r_m, ms, mr)
-    c_p = seq_copy(outg, arr, ps, pr)
-    c_e = seq_copy(rep, retd, es, er)
+    c_pa = seq_copy(outg_a, arr_a, pas, par)
+    c_pb = seq_copy(outg_b, arr_b, pbs, pbr)
+    c_ea = seq_copy(rep_a, ret_a, eas, ear)
+    c_eb = seq_copy(rep_b, ret_b, ebs, ebr)
 
     def start_all(copy, n):
         each(1, n)(lambda d: copy(d).start())
@@ -110,16 +118,17 @@
         each(1, n)(lambda d: copy(d).wait_send())
 
     half = D // 2
-    parts_right = [pl.ds(0, D)] * 3 + [pl.ds(0, half)]
-    parts_left = [pl.ds(0, D)] * 3 + [pl.ds(half, half)]
-
-    def ring_right(i):
-        ref = u_t.at[(h + HEADS - 2 * i) % HEADS, parts_right[i]]
-        return remote(ref, ref, rs.at[i], rr.at[i], "head", right)
-
-    def ring_left(i):
-        ref = u_t.at[(h + 2 * i) % HEADS, parts_left[i]]
-        return remote(ref, ref, ls.at[i], lr.at[i], "head", left)
+    first, second = pl.ds(0, half), pl.ds(half, half)
+
+    def ring_right(i, lead):
+        ref = u_t.at[(h + HEADS - 2 * i) % HEADS, first if lead else second]
+        n = 2 * i + 1 - lead
+        return remote(ref, ref, rs.at[n], rr.at[n], "head", right)
+
+    def ring_left(i, lead):
+        ref = u_t.at[(h + 2 * i) % HEADS, second if lead else first]
+        n = 2 * i + 1 - lead
+        return remote(ref, ref, ls.at[n], lr.at[n], "head", left)
 
     def to_sib(k):
         ref = u_t.at[(h + 2 * k) % HEADS]
@@ -152,31 +161,33 @@
         pair = pjv[:, 8 * HS * i : 8 * HS * (i + 1)].T
         for k in range(2):
             p_q[2 * i + k] = pair[4 * HS * k : 4 * HS * k + 3 * HS]
-            p_f[2 * i + k] = pair[4 * HS * k + 3 * HS : 4 * HS * (k + 1)]
+            p_fa[2 * i + k] = pair[4 * HS * k + 3 * HS : 4 * HS * k + 3 * HS + FEW]
+            p_fb[2 * i + k] = pair[4 * HS * k + 3 * HS + FEW : 4 * HS * (k + 1)]
     pl.semaphore_wait(barrier, HEADS + SHARDS - 2)
 
-    start_all(c_f, HEADS)
-    f_t[h] = p_f[h]
+    start_all(c_fa, HEADS)
+    start_all(c_fb, HEADS)
+    f_ta[h] = p_fa[h]
+    f_tb[h] = p_fb[h]
     q_t[h] = p_q[h]
     l_up.wait()
     for i in range(2):
         u_t[h, half * i : half * (i + 1)] = upv[:, half * i : half * (i + 1)].T
     run_t[SLOTS] = jnp.zeros((HS, BLOCK), F32)
-    run_s[TILES] = jnp.zeros((HS, BLOCK), F32)
+    run_sa[SLOTS] = jnp.zeros((MANY, BLOCK), F32)
+    run_sb[SLOTS] = jnp.zeros((FEW, BLOCK), F32)
     run_k[QB * KMAX] = jnp.zeros((HS, BLOCK), F32)
     run_v[QB * KMAX] = jnp.zeros((HS, BLOCK), F32)
 
     def ring_step(i):
-        ring_right(i - 1).wait_recv()
+        for lead in (1, 0) if i < 4 else (1,):
+            for ring in (ring_right, ring_left):
+                ring(i - 1, lead).wait_recv()
+                if i < 3 or (lead and i < 4):
+                    ring(i, lead).start()
         if i < 4:
-            ring_right(i).start()
             to_sib(8 - i).start()
-        ring_left(i - 1).wait_recv()
-        if i < 4:
-            ring_left(i).start()
-            to_sib(i).start()
-        else:
-            to_sib(4).start()
+        to_sib(i).start()
 
     for load in l_small:
         load.wait()
@@ -200,14 +211,10 @@
     mine = own_m[pl.ds(s, 1), :]
     going = first_three((mine == row) & (lane < TILES))
     coming = first_three((own_m[...] == s) & (lane < TILES))
-    slots_v[:SHARDS] = in_lanes(going, 0)
+    slots_v[:SHARDS] = in_lanes(going, -1)
     slots_v[SHARDS:] = in_lanes(coming, -1)
     l_slots = pltpu.make_async_copy(slots_v, slots, tb.at[0])
     l_slots.start()
-    rank = jnp.where(lane == going[1], 1, jnp.where(lane == going[2], 2, 0))
-    slot_of = CAP * jnp.where(lane1 < TILES, mine, 0) + jnp.max(rank, axis=0, keepdims=True)
-    chains_v[SLOT_OF : SLOT_OF + 1] = slot_of
-
     def slot_target(n, k):
         tile = slots[SHARDS + n, k]
         return tile, targets[TILES * n + jnp.maximum(tile, 0)]
@@ -233,8 +240,9 @@
         chains_v[prev_row : prev_row + 1] = prev
         chains_v[last_row : last_row + 1] = last
 
-    def source(i, j):
-        return sources[TILES * s + 4 * i + j]
+    def source(d, k):
+        tile = slots[(s + SHARDS - d) % SHARDS, k]
+        return jnp.where(tile < 0, -1, sources[TILES * s + jnp.maximum(tile, 0)])
 
     def target(i, j):
         tile, at = slot_target(i, j)
@@ -244,45 +252,58 @@
         return keys[j, (h + 1 + i) % QB]
 
     l_slots.wait()
-    recv_all(c_f, HEADS)
-    ring_right(0).start()
-    ring_left(0).start()
+    l_tw.wait()
+
+    def products(f_t, part, outg):
+        @each(0, TILES, 8)
+        def _(t):
+            part[t] = nt(f_t[sources[TILES * s + t]], twv[t]).astype(BF16)
+
+        @each(0, SHARDS, 4)
+        def _(n):
+            for k in range(CAP):
+                outg[CAP * n + k] = part[jnp.maximum(slots[n, k], 0)]
+
+    own_slots = pl.ds(s * CAP, CAP)
+    recv_all(c_fa, HEADS)
+    products(f_ta, part_a, outg_a)
+    start_all(c_pa, SHARDS)
+    recv_all(c_fb, HEADS)
+    for lead in (1, 0):
+        ring_right(0, lead).start()
+        ring_left(0, lead).start()
     to_sib(0).start()
-    l_tw.wait()
-
-    @each(0, TILES, 8)
-    def _(t):
-        part[t] = nt(f_t[sources[TILES * s + t]], twv[t]).astype(BF16)
-
-    @each(0, SHARDS, 4)
-    def _(n):
-        for k in range(CAP):
-            outg[CAP * n + k] = part[slots[n, k]]
-
-    start_all(c_p, SHARDS)
-    arr[pl.ds(s * CAP, CAP)] = outg[pl.ds(s * CAP, CAP)]
-    chain(TILES // 4, 4, source, TILES, PREV_SRC, LAST_SRC)
+    products(f_tb, part_b, outg_b)
+    start_all(c_pb, SHARDS)
+    each(1, 4)(lambda d: c_q(d).start())
+    arr_a[own_slots] = outg_a[own_slots]
+    arr_b[own_slots] = outg_b[own_slots]
+    chain(SHARDS, CAP, source, SLOTS, PREV_SRC, LAST_SRC)
     ring_step(1)
     chain(QB, KMAX, key, QB * KMAX, PREV_KEY, LAST_KEY)
     ring_step(2)
-    each(1, 5)(lambda d: c_q(d).start())
+    each(4, 8)(lambda d: c_q(d).start())
     chain(SHARDS, CAP, target, SLOTS, PREV_TGT, LAST_TGT)
     l_chains = pltpu.make_async_copy(chains_v, chains, tb.at[1])
     l_chains.start()
     ring_step(3)
-    each(5, 9)(lambda d: c_q(d).start())
+    each(8, HEADS)(lambda d: c_q(d).start())
     ring_step(4)
-    each(9, HEADS)(lambda d: c_q(d).start())
     each(0, 8)(lambda k: to_sib(k).wait_recv())
     l_chains.wait()
 
-    @each(0, SHARDS, 4)
-    def _(n):
-        for k in range(CAP):
-            rep[CAP * n + k] = u_t[slot_target(n, k)[1], my_rows]
-
-    start_all(c_e, SHARDS)
-    retd[pl.ds(s * CAP, CAP)] = rep[pl.ds(s * CAP, CAP)]
+    def replies(rep, ret, rows):
+        @each(0, SHARDS, 4)
+        def _(n):
+            for k in range(CAP):
+                rep[CAP * n + k] = u_t[slot_target(n, k)[1], rows]
+
+        ret[own_slots] = rep[own_slots]
+
+    replies(rep_a, ret_a, my_many)
+    start_all(c_ea, SHARDS)
+    replies(rep_b, ret_b, my_few)
+    start_all(c_eb, SHARDS)
 
     l_ow.wait()
 
@@ -290,11 +311,14 @@
     def _(b):
         g_t[b] = nn(owv[my_rows], u_t[b]).astype(BF16)
 
-    recv_all(c_p, SHARDS)
+    recv_all(c_pa, SHARDS)
+    recv_all(c_pb, SHARDS)
 
     @each(0, SLOTS, 8)
     def _(p):
-        run_t[p] = arr[p].astype(F32) + run_t[chains[PREV_TGT, p]]
+        before = run_t[chains[PREV_TGT, p]]
+        run_t[p, :FEW] = arr_a[p].astype(F32) + before[:FEW]
+        run_t[p, FEW:] = arr_b[p].astype(F32) + before[FEW:]
 
     @each(1, HEADS)
     def _(d):
@@ -304,6 +328,15 @@
 
     r_m[h] = run_t[chains[LAST_TGT, h]].astype(BF16)
 
+    for copy in (c_fa, c_fb):
+        send_all(copy, HEADS)
+    for copy in (c_pa, c_pb):
+        send_all(copy, SHARDS)
+    for i in range(4):
+        for lead in (1, 0) if i < 3 else (1,):
+            ring_right(i, lead).wait_send()
+            ring_left(i, lead).wait_send()
+    each(0, 8)(lambda k: to_sib(k).wait_send())
     recv_all(c_q, HEADS)
 
     @each(0, QB, 2)
@@ -354,12 +387,17 @@
             run_k[KMAX * i + j] = term_k[:, lanes] + run_k[before]
             run_v[KMAX * i + j] = term_v[:, lanes] + run_v[before]
 
-    @each(0, QB - 1)
-    def _(i):
-        attend(i)
-        c_a(i + 1).start()
-
-    attend(QB - 1)
+    @each(0, QB // 4)
+    def _(g):
+        for j in range(4):
+            attend(4 * g + j)
+        for j in range(3):
+            c_a(4 * g + j + 1).start()
+
+        @pl.when(g < QB // 4 - 1)
+        def _():
+            c_a(4 * g + 4).start()
+
     r_a[h] = s_a[h]
 
     @each(1, HEADS)
@@ -399,30 +437,39 @@
     start_all(c_x, NX)
     wx_r[x] = wg_p[pl.ds(x * NZ, NZ)]
 
+    group = 4
+
+    def back(copy, ret, run, sent):
+        def some(g, first):
+            for j in range(first, group):
+                copy(group * g + j).wait_recv()
+            for j in range(group):
+                d = group * g + j
+                n = (s + SHARDS - d) % SHARDS
+                for k in range(CAP):
+                    q = CAP * d + k
+                    term = nn(ret[CAP * n + k], twv[jnp.maximum(slots[n, k], 0)])
+                    run[q] = term + run[chains[PREV_SRC, q]]
+
+        some(0, 1)
+        each(1, SHARDS // group)(lambda g: some(g, 0))
+
+        @each(0, QB, 4)
+        def _(b):
+            sent[b] = run[chains[LAST_SRC, b]].astype(BF16)
+
+    back(c_ea, ret_a, run_sa, s_fa)
+    start_all(c_dfa, HEADS)
+    o_fa = pltpu.make_async_copy(s_fa.at[h], r_fa.at[h], out.at[1])
+    o_fa.start()
     recv_all(c_x, NX)
     wz_p[...] = wx_r[0] + wx_r[1] + wx_r[2] + wx_r[3]
     wz_r[z] = wz_p[z]
-
-    recv_all(c_e, SHARDS)
+    back(c_eb, ret_b, run_sb, s_fb)
+    start_all(c_dfb, HEADS)
+    o_fb = pltpu.make_async_copy(s_fb.at[h], r_fb.at[h], out.at[5])
+    o_fb.start()
     start_all(c_z, NZ)
-
-    @each(0, TILES, 8)
-    def _(t):
-        run_s[t] = nn(retd[chains[SLOT_OF, t]], twv[t])
-
-    @each(0, TILES, 8)
-    def _(t):
-        run_s[t] = run_s[t] + run_s[chains[PREV_SRC, t]]
-
-    @each(1, HEADS)
-    def _(d):
-        b = (h + d) % HEADS
-        s_f[b] = run_s[chains[LAST_SRC, b]].astype(BF16)
-        c_df(d).start()
-
-    s_f[h] = run_s[chains[LAST_SRC, h]].astype(BF16)
-    o_f = pltpu.make_async_copy(s_f.at[h], r_f.at[h], out.at[1])
-    o_f.start()
 
     recv_all(c_a, HEADS)
     o_q = pltpu.make_async_copy(r_a.at[:, pl.ds(HS, HS)], q_out, out.at[3])
@@ -447,34 +494,36 @@
     o_wg = pltpu.make_async_copy(wg_v, wg_out, out.at[2])
     o_wg.start()
 
+    for copy in (c_q, c_m, c_a, c_kv):
+        send_all(copy, HEADS)
+    for copy in (c_ea, c_eb):
+        send_all(copy, SHARDS)
+    send_all(c_x, NX)
     recv_all(c_kv, HEADS)
-    recv_all(c_df, HEADS)
-    for copy in (o_kv, o_f, o_wg, o_q, o_lo):
+    recv_all(c_dfa, HEADS)
+    recv_all(c_dfb, HEADS)
+    for copy in (o_kv, o_fa, o_fb, o_wg, o_q, o_lo):
         copy.wait()
 
-    for copy in (c_f, c_q, c_a, c_kv, c_df, c_m):
+    for copy in (c_dfa, c_dfb):
         send_all(copy, HEADS)
-    send_all(c_p, SHARDS)
-    send_all(c_e, SHARDS)
-    send_all(c_x, NX)
     send_all(c_z, NZ)
-    for i in range(4):
-        ring_right(i).wait_send()
-        ring_left(i).wait_send()
-    each(0, 8)(lambda k: to_sib(k).wait_send())
 
 
 def finish(
-    lo, q, kv, f, wg, lo_out, gp_out, wg_out, lo_v, q_v, kv_v, f_v, wg_v, gp_v, sem
+    lo, q, kv, fa, fb, wg, lo_out, gp_out, wg_out,
+    lo_v, q_v, kv_v, fa_v, fb_v, wg_v, gp_v, sem,
 ):
     loads = [
         pltpu.make_async_copy(a, b, sem.at[n])
-        for n, (a, b) in enumerate(((lo, lo_v), (wg, wg_v), (q, q_v), (kv, kv_v), (f, f_v)))
+        for n, (a, b) in enumerate(
+            ((lo, lo_v), (wg, wg_v), (q, q_v), (kv, kv_v), (fa, fa_v), (fb, fb_v))
+        )
     ]
     for copy in loads:
         copy.start()
     stores = [
-        pltpu.make_async_copy(a, b, sem.at[9 + n])
+        pltpu.make_async_copy(a, b, sem.at[10 + n])
         for n, (a, b) in enumerate(((lo_v, lo_out), (wg_v, wg_out)))
     ]
     for copy in loads:
@@ -485,13 +534,13 @@
     for i in range(HEADS // 2):
         rows = []
         for n in (2 * i, 2 * i + 1):
-            rows += [q_v[n], kv_v[n], f_v[n]]
+            rows += [q_v[n], kv_v[n], fa_v[n], fb_v[n]]
         lanes = pl.ds(wide * i, wide)
         gp_v[:, lanes] = jnp.concatenate(rows, axis=0).T
         if i % 2:
             lanes = pl.ds(wide * (i - 1), 2 * wide)
             stores.append(
-                pltpu.make_async_copy(gp_v.at[:, lanes], gp_out.at[:, lanes], sem.at[5 + i // 2])
+                pltpu.make_async_copy(gp_v.at[:, lanes], gp_out.at[:, lanes], sem.at[6 + i // 2])
             )
             stores[-1].start()
     for copy in stores:
@@ -513,17 +562,18 @@
     tiles = (HS, BLOCK)
     tall = jax.ShapeDtypeStruct((HEADS, *tiles), BF16)
     columns = D // SHARDS
-    lo, q, kv, f, wg = pl.pallas_call(
+    lo, q, kv, fa, fb, wg = pl.pallas_call(
         kernel,
         out_shape=(
             jax.ShapeDtypeStruct((BLOCK, D), BF16),
             tall,
             jax.ShapeDtypeStruct((HEADS, 2 * HS, BLOCK), BF16),
-            tall,
+            jax.ShapeDtypeStruct((HEADS, MANY, BLOCK), BF16),
+            jax.ShapeDtypeStruct((HEADS, FEW, BLOCK), BF16),
             jax.ShapeDtypeStruct((columns, HS), F32),
         ),
         in_specs=[any_space] * 9,
-        out_specs=(any_space,) * 5,
+        out_specs=(any_space,) * 6,
         scratch_shapes=[
             buf(1, SHARDS * TILES, dtype=jnp.int32), pltpu.SMEM((SHARDS * TILES,), jnp.int32),
             pltpu.SMEM((SHARDS * TILES,), jnp.int32), pltpu.SMEM((KMAX, QB), jnp.int32),
@@ -532,25 +582,26 @@
             pltpu.SMEM((2 * SHARDS, BLOCK), jnp.int32),
             buf(8, BLOCK, dtype=jnp.int32), pltpu.SMEM((8, BLOCK), jnp.int32),
             buf(BLOCK, 4 * D), buf(BLOCK, D), buf(D, D), buf(TILES, BLOCK, BLOCK),
-            buf(HEADS, *tiles), buf(HEADS, 3 * HS, BLOCK),
-            buf(HEADS, *tiles), buf(HEADS, 3 * HS, BLOCK),
+            buf(HEADS, FEW, BLOCK), buf(HEADS, MANY, BLOCK), buf(HEADS, 3 * HS, BLOCK),
+            buf(HEADS, FEW, BLOCK), buf(HEADS, MANY, BLOCK), buf(HEADS, 3 * HS, BLOCK),
             buf(QB, D, BLOCK), buf(QB, *tiles), buf(QB, BLOCK, 2 * HS),
-            buf(TILES, *tiles), buf(SLOTS, *tiles), buf(SLOTS, *tiles),
-            buf(SLOTS, *tiles), buf(SLOTS, *tiles),
-            buf(SLOTS + 1, *tiles, dtype=F32), buf(TILES + 1, *tiles, dtype=F32),
+            buf(TILES, FEW, BLOCK), buf(TILES, MANY, BLOCK),
+            buf(SLOTS, FEW, BLOCK), buf(SLOTS, MANY, BLOCK),
+            buf(SLOTS, FEW, BLOCK), buf(SLOTS, MANY, BLOCK),
+            buf(SLOTS, MANY, BLOCK), buf(SLOTS, FEW, BLOCK),
+            buf(SLOTS, MANY, BLOCK), buf(SLOTS, FEW, BLOCK),
+            buf(SLOTS + 1, *tiles, dtype=F32), buf(SLOTS + 1, MANY, BLOCK, dtype=F32),
+            buf(SLOTS + 1, FEW, BLOCK, dtype=F32),
             buf(QB * KMAX + 1, *tiles, dtype=F32), buf(QB * KMAX + 1, *tiles, dtype=F32),
             buf(HEADS, 2 * HS, BLOCK), buf(HEADS, 2 * HS, BLOCK),
-            buf(HEADS, *tiles), buf(HEADS, *tiles),
+            buf(HEADS, MANY, BLOCK), buf(HEADS, FEW, BLOCK), buf(HEADS, *tiles),
             buf(HEADS, 2 * HS, BLOCK), buf(HEADS, *tiles),
             buf(D, HS, dtype=F32), buf(SHARDS, D // SHARDS, HS, dtype=F32),
             buf(NX, NZ, D // SHARDS, HS, dtype=F32),
             buf(NZ, D // SHARDS, HS, dtype=F32), buf(NZ, D // SHARDS, HS, dtype=F32),
-            sems(9), sems(2), sems(5), sems(HEADS), sems(HEADS), sems(HEADS), sems(HEADS),
-            sems(4), sems(4), sems(4), sems(4), sems(8), sems(8),
-            sems(SHARDS), sems(SHARDS), sems(SHARDS), sems(SHARDS),
-            sems(HEADS), sems(HEADS), sems(HEADS), sems(HEADS),
-            sems(HEADS), sems(HEADS), sems(HEADS), sems(HEADS),
-            sems(NX), sems(NX), sems(NZ), sems(NZ),
+            sems(9), sems(2), sems(6), *[sems(HEADS)] * 6,
+            sems(7), sems(7), sems(7), sems(7), sems(8), sems(8), *[sems(SHARDS)] * 8,
+            *[sems(HEADS)] * 10, sems(NX), sems(NX), sems(NZ), sems(NZ),
         ],
         compiler_params=pltpu.CompilerParams(
             collective_id=0, has_side_effects=True, vmem_limit_bytes=61 << 20
@@ -566,14 +617,14 @@
             jax.ShapeDtypeStruct((BLOCK, 4 * D), BF16),
             jax.ShapeDtypeStruct((columns, HS), F32),
         ),
-        in_specs=[any_space] * 5,
+        in_specs=[any_space] * 6,
         out_specs=(any_space,) * 3,
         scratch_shapes=[
-            buf(BLOCK, D), buf(HEADS, *tiles), buf(HEADS, 2 * HS, BLOCK), buf(HEADS, *tiles),
-            buf(columns, HS, dtype=F32), buf(BLOCK, 4 * D), sems(11),
+            buf(BLOCK, D), buf(HEADS, *tiles), buf(HEADS, 2 * HS, BLOCK), buf(HEADS, MANY, BLOCK),
+            buf(HEADS, FEW, BLOCK), buf(columns, HS, dtype=F32), buf(BLOCK, 4 * D), sems(12),
         ],
         compiler_params=pltpu.CompilerParams(vmem_limit_bytes=61 << 20),
-    )(lo, q, kv, f, wg)
+    )(lo, q, kv, fa, fb, wg)
     return layer_out, grad_projected, weight_grad.T
 
 

time: 100 us -> 97.1 us (0.971)
  Pallas kernels: 99.5 us -> 96.2 us
    pallas_call x1, Pallas kernels: 97.1 us -> 93.9 us  [body(): pl.pallas_call(kernel, out_shape=(jax.ShapeDtypeStruct((BLOCK, D), BF16),...]
where the time goes in v3:
time: 97.1 us; the launch traced here: 96.9 us
  Pallas kernels  96.2 us (99%)
    pallas_call x1, Pallas kernels, body(): pl.pallas_call(kernel, out_shape=(jax.ShapeDtypeStruct((BLOCK, D), BF16),...  93.9 us
    pallas_call x1, Pallas kernels, body(): pl.pallas_call(finish, out_shape=(jax.ShapeDtypeStruct((BLOCK, D), BF16),...  2.32 us

profile of v3, /device:TPU:1, one launch (start us, length us, event | category | flops | bytes accessed | tf_op | source)
XLA Modules:
  0.0 96.9 jit_solution(5934895432576052797)
XLA Ops:
  0.6 93.9 %shard_map.112 = (bf16[128,768]{1,0:T(8,128)(2,1)}, bf16[16,48,128]{2,1,0:T(8,128)(2,1)}, bf16[16,96,128]{2,1,0:T(8,128)(2,1)}, bf16[16,32,128]{2,1,0:T(8,128)(2...) custom-call(s32[1,1536]{1,0:T(1,128)} %bitcast.3, s32[1536]{0:T(1024)} %sources_in.1, s32[1536]{0:T(1024)} %targets_in.1, ...), custom_call_target="tpu_custom_call" | custom-call | tf_op jit(solution)/shard_map/pallas_call | solution.py:565
  94.6 2.3 %shard_map.113 = (bf16[128,768]{1,0:T(8,128)(2,1)}, bf16[128,3072]{1,0:T(8,128)(2,1)}, f32[24,48]{1,0:T(8,128)}) custom-call(bf16[128,768]{1,0:T(8,128)(2,1)} %get-tuple-element.12.lo, bf16[16,48,128]{2,1,0:T(8,128)(2,1)} %get-tuple-element.13.q, bf16[16,96,128]{2,1,0:T(8,128)(2,1)} %get-tuple-element.14.kv, bf16[16,32,128]{2,1,0:T(8,128)(2,1)} %get-tuple-element.15.fa, ...), custom_call_target="tpu_custom_call" | custom-call | tf_op jit(solution)/shard_map/pallas_call | solution.py:613

commit v4 on v3

--- a/solution.py
+++ b/solution.py
@@ -189,6 +189,10 @@
             to_sib(8 - i).start()
         to_sib(i).start()
 
+    for lead in (1, 0):
+        ring_right(0, lead).start()
+        ring_left(0, lead).start()
+    to_sib(0).start()
     for load in l_small:
         load.wait()
     for n in range(SHARDS):
@@ -269,17 +273,13 @@
     products(f_ta, part_a, outg_a)
     start_all(c_pa, SHARDS)
     recv_all(c_fb, HEADS)
-    for lead in (1, 0):
-        ring_right(0, lead).start()
-        ring_left(0, lead).start()
-    to_sib(0).start()
+    ring_step(1)
     products(f_tb, part_b, outg_b)
     start_all(c_pb, SHARDS)
     each(1, 4)(lambda d: c_q(d).start())
     arr_a[own_slots] = outg_a[own_slots]
     arr_b[own_slots] = outg_b[own_slots]
     chain(SHARDS, CAP, source, SLOTS, PREV_SRC, LAST_SRC)
-    ring_step(1)
     chain(QB, KMAX, key, QB * KMAX, PREV_KEY, LAST_KEY)
     ring_step(2)
     each(4, 8)(lambda d: c_q(d).start())
@@ -462,13 +462,13 @@
     start_all(c_dfa, HEADS)
     o_fa = pltpu.make_async_copy(s_fa.at[h], r_fa.at[h], out.at[1])
     o_fa.start()
-    recv_all(c_x, NX)
-    wz_p[...] = wx_r[0] + wx_r[1] + wx_r[2] + wx_r[3]
-    wz_r[z] = wz_p[z]
     back(c_eb, ret_b, run_sb, s_fb)
     start_all(c_dfb, HEADS)
     o_fb = pltpu.make_async_copy(s_fb.at[h], r_fb.at[h], out.at[5])
     o_fb.start()
+    recv_all(c_x, NX)
+    wz_p[...] = wx_r[0] + wx_r[1] + wx_r[2] + wx_r[3]
+    wz_r[z] = wz_p[z]
     start_all(c_z, NZ)
 
     recv_all(c_a, HEADS)

time: 97.1 us -> 95 us (0.978)
  Pallas kernels: 96.2 us -> 94.1 us
    pallas_call x1, Pallas kernels: 93.9 us -> 91.8 us  [body(): pl.pallas_call(kernel, out_shape=(jax.ShapeDtypeStruct((BLOCK, D), BF16),...]
where the time goes in v4:
time: 95 us; the launch traced here: 94.8 us
  Pallas kernels  94.1 us (99%)
    pallas_call x1, Pallas kernels, body(): pl.pallas_call(kernel, out_shape=(jax.ShapeDtypeStruct((BLOCK, D), BF16),...  91.8 us
    pallas_call x1, Pallas kernels, body(): pl.pallas_call(finish, out_shape=(jax.ShapeDtypeStruct((BLOCK, D), BF16),...  2.32 us

profile of v4, /device:TPU:1, one launch (start us, length us, event | category | flops | bytes accessed | tf_op | source)
XLA Modules:
  0.0 94.8 jit_solution(14895369100632117370)
XLA Ops:
  0.6 91.8 %shard_map.112 = (bf16[128,768]{1,0:T(8,128)(2,1)}, bf16[16,48,128]{2,1,0:T(8,128)(2,1)}, bf16[16,96,128]{2,1,0:T(8,128)(2,1)}, bf16[16,32,128]{2,1,0:T(8,128)(2...) custom-call(s32[1,1536]{1,0:T(1,128)} %bitcast.3, s32[1536]{0:T(1024)} %sources_in.1, s32[1536]{0:T(1024)} %targets_in.1, ...), custom_call_target="tpu_custom_call" | custom-call | tf_op jit(solution)/shard_map/pallas_call | solution.py:565
  92.4 2.3 %shard_map.113 = (bf16[128,768]{1,0:T(8,128)(2,1)}, bf16[128,3072]{1,0:T(8,128)(2,1)}, f32[24,48]{1,0:T(8,128)}) custom-call(bf16[128,768]{1,0:T(8,128)(2,1)} %get-tuple-element.12.lo, bf16[16,48,128]{2,1,0:T(8,128)(2,1)} %get-tuple-element.13.q, bf16[16,96,128]{2,1,0:T(8,128)(2,1)} %get-tuple-element.14.kv, bf16[16,32,128]{2,1,0:T(8,128)(2,1)} %get-tuple-element.15.fa, ...), custom_call_target="tpu_custom_call" | custom-call | tf_op jit(solution)/shard_map/pallas_call | solution.py:613

commit v5 on v4

--- a/solution.py
+++ b/solution.py
@@ -279,10 +279,10 @@
     each(1, 4)(lambda d: c_q(d).start())
     arr_a[own_slots] = outg_a[own_slots]
     arr_b[own_slots] = outg_b[own_slots]
+    ring_step(2)
+    each(4, 8)(lambda d: c_q(d).start())
     chain(SHARDS, CAP, source, SLOTS, PREV_SRC, LAST_SRC)
     chain(QB, KMAX, key, QB * KMAX, PREV_KEY, LAST_KEY)
-    ring_step(2)
-    each(4, 8)(lambda d: c_q(d).start())
     chain(SHARDS, CAP, target, SLOTS, PREV_TGT, LAST_TGT)
     l_chains = pltpu.make_async_copy(chains_v, chains, tb.at[1])
     l_chains.start()

time: 95 us -> 95 us (level)
  no operation moved by 1% of the time
where the time goes in v5:
time: 95 us; the launch traced here: 94.8 us
  Pallas kernels  94.2 us (99%)
    pallas_call x1, Pallas kernels, body(): pl.pallas_call(kernel, out_shape=(jax.ShapeDtypeStruct((BLOCK, D), BF16),...  91.9 us
    pallas_call x1, Pallas kernels, body(): pl.pallas_call(finish, out_shape=(jax.ShapeDtypeStruct((BLOCK, D), BF16),...  2.32 us

profile of v5, /device:TPU:1, one launch (start us, length us, event | category | flops | bytes accessed | tf_op | source)
XLA Modules:
  0.0 94.8 jit_solution(11398614521241548430)
XLA Ops:
  0.6 91.9 %shard_map.112 = (bf16[128,768]{1,0:T(8,128)(2,1)}, bf16[16,48,128]{2,1,0:T(8,128)(2,1)}, bf16[16,96,128]{2,1,0:T(8,128)(2,1)}, bf16[16,32,128]{2,1,0:T(8,128)(2...) custom-call(s32[1,1536]{1,0:T(1,128)} %bitcast.3, s32[1536]{0:T(1024)} %sources_in.1, s32[1536]{0:T(1024)} %targets_in.1, ...), custom_call_target="tpu_custom_call" | custom-call | tf_op jit(solution)/shard_map/pallas_call | solution.py:565
  92.5 2.3 %shard_map.113 = (bf16[128,768]{1,0:T(8,128)(2,1)}, bf16[128,3072]{1,0:T(8,128)(2,1)}, f32[24,48]{1,0:T(8,128)}) custom-call(bf16[128,768]{1,0:T(8,128)(2,1)} %get-tuple-element.12.lo, bf16[16,48,128]{2,1,0:T(8,128)(2,1)} %get-tuple-element.13.q, bf16[16,96,128]{2,1,0:T(8,128)(2,1)} %get-tuple-element.14.kv, bf16[16,32,128]{2,1,0:T(8,128)(2,1)} %get-tuple-element.15.fa, ...), custom_call_target="tpu_custom_call" | custom-call | tf_op jit(solution)/shard_map/pallas_call | solution.py:613
